TPU v7x, 512 devices: a whole 4x8x8 slice. The times are simulated.
512 devices in a mesh: req: 32 (over x, y_lo, core), mp: 16 (over z, y_hi).
Axes of the slice: x: 4, y: 8 (y_hi: 2, y_lo: 4; y = y_hi * 4 + y_lo), z: 8, core: 2. Of those that a mesh axis runs over, the one named last changes fastest.
Arguments:
- xin: bfloat16 [32, 64, 8192], P('req', None, 'mp'), may hold values from -6 to 6
- zin: bfloat16 [32, 64, 8192], P('req', None, 'mp'), may hold values from -6 to 6
- conv_w: float32 [4, 8192], P(None, 'mp'), may hold values from -3 to 3
- conv_bias: float32 [8192], P('mp'), may hold values from -3 to 3
- x_proj: bfloat16 [8192, 288], P('mp'), may hold values from -0.0625 to 0.0625
- dt_proj: bfloat16 [256, 8192], P(None, 'mp'), may hold values from -0.375 to 0.375
- dt_bias: float32 [8192], P('mp'), may hold values from -5 to -2
- a_log: float32 [16, 8192], P(None, 'mp'), may hold values from 0 to 2.8
- d_skip: float32 [8192], P('mp'), may hold values from 0.5 to 1.5
- conv_cache: float32 [64, 3, 8192], P('req', None, 'mp'), may hold values from -6 to 6
- ssm_cache: float32 [64, 16, 8192], P('req', None, 'mp'), may hold values from -3 to 3
- prefix_of: int32 [32], replicated, may hold values from 0 to 63, as said below
- out_w: bfloat16 [8192, 4096], P('mp', 'req'), may hold values from -0.0625 to 0.0625
- resid: bfloat16 [2048, 4096], P(('req', 'mp')), may hold values from -6 to 6
- norm_gain: float32 [4096], replicated, may hold values from 0.5 to 1.5
- expert_ids: int32 [2048, 2], P('req'), may hold values from 0 to 7, all different within a row; in each aligned block of 4 rows (0 to 3, 4 to 7, ...) at most 2 rows name the same one
- gate_w: bfloat16 [2048, 2], P('req'), may hold values from 0.19921875 to 1
- w_gate: bfloat16 [32, 4096, 4096], P('req', None, 'mp'), may hold values from -0.09375 to 0.09375
- w_up: bfloat16 [32, 4096, 4096], P('req', None, 'mp'), may hold values from -0.09375 to 0.09375
Outputs:
- stream: bfloat16 [2048, 4096], P(('req', 'mp'))
- final_state: float32 [32, 16, 8192], P('req', None, 'mp')
- expert_act: bfloat16 [32, 1024, 4096], P('req', None, 'mp')
Inputs may be any that keep to these rules, and one draw needn't show every extreme that they name: `prefix_of`: prefix p is cached on index p // 2 of req. `expert_ids`: within each aligned block of 4 tokens no expert is named more than 2 times; a token's two experts differ.
All inputs are finite; a program needn't handle non-finite values.
Results may differ from a plain program's by a relative error of at most 0.025.
Values may be sent and summed in bfloat16 or wider, within the bound.
A program may use at most 64 MiB of HBM per device.

v0:
```python
import jax
import jax.numpy as jnp
from jax import lax
from jax.sharding import PartitionSpec as P

EXPERTS = 8


def slot_ranks(ids_rows):
    onehot = (ids_rows[..., None] == jnp.arange(EXPERTS, dtype=jnp.int32)).astype(jnp.int32)
    before = jnp.cumsum(onehot, axis=1) - onehot
    return jnp.sum(before * onehot, axis=-1)


def expert_hidden(slots_x, slots_g, weight_gate, weight_up):
    leading = slots_x.shape[:-1]
    flat = slots_x.reshape(-1, slots_x.shape[-1])
    gflat = slots_g.reshape(-1).astype(jnp.float32)
    gate_part = jnp.dot(flat, weight_gate, preferred_element_type=jnp.float32)
    up_part = jnp.dot(flat, weight_up, preferred_element_type=jnp.float32)
    result = (jax.nn.silu(gate_part) * up_part * gflat[:, None]).astype(jnp.bfloat16)
    return result.reshape(leading + (weight_gate.shape[1],))


def build_slots(normed, ids_rows, gate_rows, block_count, capacity):
    flat_ids = ids_rows.reshape(block_count, -1)
    ranks = slot_ranks(flat_ids)
    block_index = jnp.arange(block_count, dtype=jnp.int32)[:, None]
    positions = ((flat_ids * block_count + block_index) * capacity + ranks).reshape(-1)
    total_slots = EXPERTS * block_count * capacity
    select = (jnp.arange(total_slots, dtype=jnp.int32)[:, None] == positions[None, :]).astype(
        jnp.bfloat16
    )
    rows = jnp.repeat(normed, 2, axis=0)
    slots_x = jnp.dot(select, rows, preferred_element_type=jnp.float32).astype(jnp.bfloat16)
    slots_g = jnp.dot(select, gate_rows.reshape(-1, 1), preferred_element_type=jnp.float32).astype(
        jnp.bfloat16
    )
    return (
        slots_x.reshape(EXPERTS, block_count, capacity, -1),
        slots_g.reshape(EXPERTS, block_count, capacity),
    )


def local(
    xin,
    zin,
    conv_w,
    conv_bias,
    x_proj,
    dt_proj,
    dt_bias,
    a_log,
    d_skip,
    conv_cache,
    ssm_cache,
    prefix_of,
    out_w,
    resid,
    norm_gain,
    expert_ids,
    gate_w,
    w_gate,
    w_up,
):
    n_req = lax.axis_size("req")
    n_mp = lax.axis_size("mp")
    my_req = lax.axis_index("req")
    my_mp = lax.axis_index("mp")
    seq = xin.shape[1]
    taps = conv_w.shape[0]
    per_block = seq // n_mp
    capacity = max(2, per_block // 2)
    group = n_req // EXPERTS
    wanted = lax.dynamic_index_in_dim(prefix_of, my_req, 0, False)
    every_conv, every_state = (
        lax.all_gather(conv_cache.astype(jnp.bfloat16), "req", axis=0, tiled=True).astype(
            conv_cache.dtype
        ),
        lax.all_gather(ssm_cache.astype(jnp.bfloat16), "req", axis=0, tiled=True).astype(
            ssm_cache.dtype
        ),
    )
    conv_state = lax.dynamic_index_in_dim(every_conv, wanted, 0, False)
    start_state = lax.dynamic_index_in_dim(every_state, wanted, 0, False)
    xpad = jnp.concatenate([conv_state, xin[0].astype(jnp.float32)], axis=0)
    total = conv_w[0] * xpad[0:seq]
    for tap in range(1, taps):
        total = total + conv_w[tap] * xpad[tap : tap + seq]
    conv = total + conv_bias
    u_act = jax.nn.silu(conv).astype(jnp.bfloat16)
    dbc = lax.psum(jnp.dot(u_act, x_proj, preferred_element_type=jnp.float32), "mp")
    rank_width = dt_proj.shape[0]
    states = a_log.shape[0]
    dtin = dbc[:, :rank_width].astype(jnp.bfloat16)
    step_size = jax.nn.softplus(
        jnp.dot(dtin, dt_proj, preferred_element_type=jnp.float32) + dt_bias
    )
    b_coef = dbc[:, rank_width : rank_width + states]
    c_coef = dbc[:, rank_width + states :]
    amat = -jnp.exp(a_log)
    u_float = u_act.astype(jnp.float32)

    def advance(state, inputs):
        dt_now, b_now, c_now, u_now = inputs
        decay = jnp.exp(dt_now[None, :] * amat)
        state = decay * state + b_now[:, None] * (dt_now * u_now)[None, :]
        out_now = jnp.sum(c_now[:, None] * state, axis=0) + d_skip * u_now
        return (state, out_now)

    last_state, yv = lax.scan(advance, start_state, (step_size, b_coef, c_coef, u_float))
    ymix = (yv * jax.nn.silu(zin[0].astype(jnp.float32))).astype(jnp.bfloat16)
    partial_out = jnp.dot(
        ymix, lax.all_gather(out_w, "req", axis=1, tiled=True), preferred_element_type=jnp.float32
    )
    weight_gate = w_gate[0]
    weight_up = w_up[0]
    hidden = lax.psum_scatter(
        partial_out.astype(jnp.bfloat16), "mp", scatter_dimension=0, tiled=True
    ).astype(jnp.float32) + resid.astype(jnp.float32)
    stream = hidden.astype(jnp.bfloat16)
    normed = (
        hidden * lax.rsqrt(jnp.mean(hidden * hidden, axis=-1, keepdims=True) + 1e-05) * norm_gain
    ).astype(jnp.bfloat16)
    ids_block = lax.dynamic_slice_in_dim(expert_ids, my_mp * per_block, per_block, 0)
    gates_block = lax.dynamic_slice_in_dim(gate_w, my_mp * per_block, per_block, 0)
    slots_x, slots_g = build_slots(normed, ids_block, gates_block, 1, capacity)
    send_x = jnp.repeat(slots_x.reshape(EXPERTS, capacity, -1), group, axis=0)
    send_g = jnp.repeat(slots_g.reshape(EXPERTS, capacity), group, axis=0)
    got_x, got_g = (
        lax.all_to_all(send_x, "req", split_axis=0, concat_axis=0, tiled=True),
        lax.all_to_all(send_g, "req", split_axis=0, concat_axis=0, tiled=True),
    )
    pieces = lax.all_gather((got_x, got_g), "mp", axis=1, tiled=True)
    acts = expert_hidden(pieces[0], pieces[1], weight_gate, weight_up)
    expert_act = acts.reshape(1, -1, acts.shape[-1])
    return (stream, last_state[None], expert_act)


def solution(mesh):
    placed = (
        P("req", None, "mp"),
        P("req", None, "mp"),
        P(None, "mp"),
        P("mp"),
        P("mp", None),
        P(None, "mp"),
        P("mp"),
        P(None, "mp"),
        P("mp"),
        P("req", None, "mp"),
        P("req", None, "mp"),
        P(),
        P("mp", "req"),
        P(("req", "mp"), None),
        P(),
        P("req", None),
        P("req", None),
        P("req", None, "mp"),
        P("req", None, "mp"),
    )
    return jax.shard_map(
        local,
        mesh=mesh,
        in_specs=placed,
        out_specs=(P(("req", "mp"), None), P("req", None, "mp"), P("req", None, "mp")),
        check_vma=False,
    )
```

profile of v0, /device:TPU:1, one launch (start us, length us, event | category | flops | bytes accessed | tf_op | source)
XLA Modules:
  0.0 758.2 jit_solution(3038454150076901960)
XLA Ops:
  8.1 1.4 dynamic_slice.32
  10.7 0.9 bitcast_convert_fusion
  11.6 0.9 fusion.44
  13.2 45.8 %all_gather.16 = bf16[64,3,512]{2,1,0:T(4,128)(2,1)S(1)} all-gather(bf16[2,3,512]{2,1,0:T(4,128)(2,1)S(1)} %copy.64), channel_id=1, replica_groups=mesh['req'=32,'mp'=16] {'req'}, dimensions={0}, use_global_device_ids=true | all-gather | bytes 202752 | tf_op jit(solution)/shard_map/all_gather | solution.py:77
  59.7 0.8 fusion.42
  60.5 1.8 fusion.45
  62.4 1.5 convert_element_type.85
  66.2 183.0 %all-reduce.4.cloned.1.call-done = f32[64,288]{1,0:T(8,128)} async-done(((f32[64,288]{1,0:T(8,128)}), f32[64,288]{1,0:T(8,128)}) %all-reduce.4.cloned.1.call-update) | async-done | bytes 73744 | tf_op jit(solution)/shard_map/psum | solution.py:92
  249.2 0.9 fusion.43
  250.1 1.2 compare_select_fusion
  252.1 57.5 %while.13 = (s32[]{:T(128)}, f32[16,512]{1,0:T(8,128)S(1)}, f32[64,512]{1,0:T(8,128)S(1)}, f32[64,512]{1,0:T(8,128)S(1)}, f32[16,512]{1,0:T(8,128)S(1)}, /*index...) while((s32[]{:T(128)}, f32[16,512]{1,0:T(8,128)S(1)}, ...), condition=%wide.region_3.4_spmd.clone, body=%wide.region_1.3_spmd.sunk.clone | while | flops 50178 | bytes 125429 | solution.py:111
  309.6 3.9 convolution_convert_fusion
  313.7 1.3 dynamic-slice
  315.8 193.2 %all-reduce.6.cloned.1.call-done = bf16[64,4096]{1,0:T(8,128)(2,1)} async-done(((bf16[64,4096]{1,0:T(8,128)(2,1)}), bf16[64,4096]{1,0:T(8,128)(2,1)}) %all-reduce.6.cloned.1.call-update) | async-done | bytes 524304
  509.0 1.0 multiply_reduce_fusion.1
  510.0 1.5 multiply_convert_fusion.1
  512.3 32.9 %all_to_all.17 = bf16[32,2,4096]{2,1,0:T(2,128)(2,1)S(1)} all-to-all(bf16[32,2,4096]{2,1,0:T(2,128)(2,1)S(1)} %bitcast.79), channel_id=1, replica_groups=mesh['req'=32,'mp'=16] {'req'}, dimensions={0} | all-to-all | bytes 1048576 | tf_op jit(solution)/shard_map/all_to_all | solution.py:131
  545.2 1.1 copy.66
  547.2 10.7 %all_to_all.18 = bf16[32,1,2]{2,1,0:T(2,128)(2,1)S(1)} all-to-all(bf16[32,1,2]{2,1,0:T(2,128)(2,1)S(1)} %copy.70), channel_id=1, replica_groups=mesh['req'=32,'mp'=16] {'req'}, dimensions={0} | all-to-all | bytes 256 | tf_op jit(solution)/shard_map/all_to_all | solution.py:132
  558.0 43.5 %all-gather = bf16[32,1,32]{0,1,2:T(2,128)(2,1)S(1)} all-gather(bf16[32,1,2]{0,1,2:T(2,128)(2,1)S(1)} %copy.71), channel_id=2, replica_groups=mesh['req'=32,'mp'=16] {'mp'}, dimensions={2}, use_global_device_ids=true | all-gather | bytes 2176 | tf_op jit(solution)/shard_map/all_gather | solution.py:134
  601.7 128.7 %all-gather.9.cloned.1.call-done = bf16[32,32,4096]{2,0,1:T(8,128)(2,1)} async-done(((bf16[32,2,4096]{2,0,1:T(8,128)(2,1)}), bf16[32,32,4096]{2,0,1:T(8,128)(2,1)}) %all-gather.9.cloned.1.call-update) | async-done | bytes 8388624 | tf_op jit(solution)/shard_map/all_gather | solution.py:134
  730.4 11.2 %copy.67 = bf16[32,32,4096]{2,1,0:T(8,128)(2,1)} copy(bf16[32,32,4096]{2,0,1:T(8,128)(2,1)} %all-gather.9.cloned.1.call-done) | data formatting | bytes 16777216 | tf_op jit(solution)/shard_map/all_gather | solution.py:134
  741.6 5.9 fusion.5
  748.0 3.2 fusion.16
  (377 shorter events, 61.7 us)
Async XLA Ops:
  8.0 733.6 %copy-start = (bf16[1,4096,256]{2,1,0:T(8,128)(2,1)S(1)}, bf16[1,4096,256]{2,1,0:T(8,128)(2,1)}, u32[]{:S(2)}) copy-start(bf16[1,4096,256]{2,1,0:T(8,128)(2,1)} %param.38) | copy-start | bytes 6291460
  8.0 241.2 %all-reduce.4.cloned.1.call-start = ((), (), s32[]{:S(2)}) async-start(), calls=%async_computation.3 | async-start | bytes 196608 | tf_op jit(solution)/shard_map/psum | solution.py:92
  59.0 450.0 %copy-start.3 = (bf16[4,4096]{1,0:T(4,128)(2,1)S(1)}, bf16[4,4096]{1,0:T(4,128)(2,1)}, u32[]{:S(2)}) copy-start(bf16[4,4096]{1,0:T(4,128)(2,1)} %param.34) | copy-start | bytes 98308
  59.6 450.4 %copy-start.4 = (f32[4096]{0:T(1024)S(1)}, f32[4096]{0:T(1024)}, u32[]{:S(2)}) copy-start(f32[4096]{0:T(1024)} %param.35) | copy-start | bytes 49156
  62.3 189.0 %all-gather.5.cloned.1.call-start = ((), (), s32[]{:S(2)}) async-start(), calls=%async_computation.2 | async-start | bytes 1081344 | tf_op jit(solution)/shard_map/all_gather | solution.py:80
  63.8 245.8 %all-gather.7.cloned.1.call-start = ((), (), s32[]{:S(2)}) async-start(), calls=%async_computation.4 | async-start | bytes 4325376 | tf_op jit(solution)/shard_map/all_gather | solution.py:114
  64.4 444.6 %all-reduce.6.cloned.1.call-start = ((), (), s32[]{:S(2)}) async-start(), calls=%async_computation.6 | async-start | bytes 1048576
  309.6 236.7 %copy-start.2 = (f32[16,512]{1,0:T(8,128)}, f32[16,512]{1,0:T(8,128)S(1)}, u32[]{:S(2)}) copy-start(f32[16,512]{1,0:T(8,128)S(1)} %get-tuple-element.52) | copy-start | bytes 98308
  309.6 236.7 %copy-start.6 = (bf16[64,2]{0,1:T(2,128)(2,1)S(1)}, bf16[64,2]{0,1:T(2,128)(2,1)}, u32[]{:S(2)}) copy-start(bf16[64,2]{0,1:T(2,128)(2,1)} %param.37) | copy-start | bytes 772
  313.5 416.9 %all-gather.9.cloned.1.call-start = ((), (), s32[]{:S(2)}) async-start(), calls=%async_computation.5 | async-start | bytes 8912896 | tf_op jit(solution)/shard_map/all_gather | solution.py:134
  741.6 5.9 copy-start.1
  741.6 6.4 copy-start.5
Sparse Core Ops, SparseCore 0:
  62.4 186.7 all-reduce.3
  313.6 195.3 all-reduce.5
  546.4 183.8 all-gather.8
Sparse Core Ops, SparseCore 1:
  65.7 61.2 all-gather.4
  129.1 72.8 all-gather.6
where the time goes:
time: 765 us; the launch traced here: 758 us
  waiting for transfers between devices  506 us (66%)
  blocking collectives  133 us (17%)
  other arithmetic  59.5 us (8%)
  local copies, waits for them, and re-layouts  23.4 us (3%)
  between operations  18 us (2%)
  matrix products  16.2 us (2%)
    unnamed x6, waiting for transfers between devices  194 us
    psum x1, waiting for transfers between devices, local(): lax.psum(jnp.dot(u_act, x_proj, preferred_element_type=jnp.float32), 'mp')  183 us
    all_gather x1, waiting for transfers between devices, local(): pieces = lax.all_gather((got_x, got_g), 'mp', axis=1, tiled=True)  129 us
    all_gather x1, blocking collectives, local(): lax.all_gather(conv_cache.astype(jnp.bfloat16), 'req', axis=0, tiled=True)  45.8 us
    add x64, other arithmetic, advance(): out_now = jnp.sum(c_now[:, None] * state, axis=0) + d_skip * u_now  44.5 us
    all_gather x1, blocking collectives, local(): pieces = lax.all_gather((got_x, got_g), 'mp', axis=1, tiled=True)  43.5 us
    all_to_all x1, blocking collectives, local(): lax.all_to_all(send_x, 'req', split_axis=0, concat_axis=0, tiled=True)  32.9 us
  transfers between devices with their start and end apart: 5, of which 3 were waited for; matrix products, arithmetic and copies ran while one was open for 8% of the time, Pallas kernels for 0%

commit v1 on v0

v1 whole, which is shorter than its diff:
```python
import jax
import jax.numpy as jnp
from jax import lax
from jax.experimental import pallas as pl
from jax.experimental.pallas import tpu as pltpu
from jax.sharding import PartitionSpec as P

F32 = jnp.float32
BF16 = jnp.bfloat16
MESH = pl.DeviceIdType.MESH

D = 4096
CH = 512
NS = 16
SUF = 64
DTR = 256
EXPERTS = 8
HID = 256
KT = 1024


def iota(shape, dim):
    return lax.broadcasted_iota(jnp.int32, shape, dim)


def silu(v):
    return v / (1.0 + jnp.exp(-v))


def steps_right(g):
    return 4 if g < 2 else 3


def steps_left(g):
    return 3 if g < 2 else 4


def kernel(
    prefix_of,
    xin,
    zin,
    conv_w,
    conv_bias,
    x_proj,
    dt_proj,
    dt_bias,
    a_log,
    d_skip,
    conv_cache,
    ssm_cache,
    out_w,
    resid,
    norm_gain,
    expert_ids,
    gate_w,
    w_gate,
    w_up,
    stream_out,
    state_out,
    act_out,
    cc16,
    cs16,
    xpad,
    a_send,
    a_recv1,
    a_mid,
    a_recv2,
    b_send,
    b_recv1,
    b_mid,
    b_recv2,
    gmat,
    d_send,
    d_recv,
    d_sum,
    d_all,
    dt_s,
    u_s,
    yv_s,
    b_exp,
    c_exp,
    ow,
    pq,
    perm_big,
    perm_small,
    p_send,
    p_recv,
    r4,
    r32,
    h4,
    sel,
    e_send,
    e_mid,
    e_recv,
    xb,
    wg,
    wu,
    acc_g,
    acc_u,
    s_a1,
    r_a1,
    s_a2,
    r_a2,
    s_b1,
    r_b1,
    s_b2,
    r_b2,
    s_d1,
    r_d1,
    s_d2,
    r_d2,
    s_oy,
    r_oy,
    s_ox,
    r_ox,
    s_ox2,
    r_ox2,
    s_os,
    r_os,
    s_p,
    r_p,
    s_ex,
    r_ex,
    s_ey,
    r_ey,
    s_zr,
    r_zr,
    s_zs,
    r_zs,
    loc,
):
    me = lax.axis_index("req")
    mp = lax.axis_index("mp")
    x = me // 8
    ylo = (me // 2) % 4
    core = me % 2
    j = me % 8
    z = mp // 2
    hi = mp % 2
    yy = hi * 4 + ylo

    def req_of(px, pylo, pcore):
        return px * 8 + pylo * 2 + pcore

    def send(src, dst, ssem, rsem, to_req, to_mp):
        return pltpu.make_async_remote_copy(
            src_ref=src,
            dst_ref=dst,
            send_sem=ssem,
            recv_sem=rsem,
            device_id=(to_req, to_mp),
            device_id_type=MESH,
        )

    pending = []

    def go(copy):
        copy.start()
        pending.append(copy)
        return copy

    x_to = {d: req_of((x + d) % 4, ylo, core) for d in (1, 2, 3)}
    j_to = {d: x * 8 + (j + d) % 8 for d in range(1, 8)}
    mp_to = {}
    for dz in range(8):
        for dh in range(2):
            if dz or dh:
                mp_to[dz * 2 + dh] = ((z + dz) % 8) * 2 + (hi + dh) % 2
    y_to = {}
    for d in range(1, 8):
        other = (yy + d) % 8
        y_to[d] = (req_of(x, other % 4, core), z * 2 + other // 4)
    sibling = req_of(x, ylo, 1 - core)

    barrier = pltpu.get_barrier_semaphore()
    count = 0
    for d in (1, 2, 3):
        pl.semaphore_signal(barrier, inc=1, device_id=(x_to[d], mp), device_id_type=MESH)
        count += 1
    for d in range(1, 8):
        pl.semaphore_signal(barrier, inc=1, device_id=(j_to[d], mp), device_id_type=MESH)
        count += 1
    for d in mp_to:
        pl.semaphore_signal(barrier, inc=1, device_id=(me, mp_to[d]), device_id_type=MESH)
        count += 1
    for d in (1, 2, 3):
        to = req_of(x, (ylo + d) % 4, core)
        pl.semaphore_signal(
            barrier, inc=1, device_id=(to, z * 2 + (1 - hi)), device_id_type=MESH
        )
        count += 1

    own_id = core * 16 + x * 4 + ylo
    load_g = pltpu.make_async_copy(w_gate.at[0], wg, loc.at[0])
    load_u = pltpu.make_async_copy(w_up.at[0], wu, loc.at[1])
    load_o = pltpu.make_async_copy(out_w, ow.at[own_id], loc.at[2])
    load_g.start()
    load_u.start()
    load_o.start()

    cc16[...] = jnp.zeros_like(cc16)
    for s in range(2):
        for k in range(3):
            for q in range(4):
                cc16[s, 4 * k + q : 4 * k + q + 1, :] = conv_cache[s, k : k + 1, q * 128 : q * 128 + 128]

    def fill_a(t, _):
        p = prefix_of[t]
        f0 = jnp.where(p == 2 * me, 1.0, 0.0).astype(F32)
        f1 = jnp.where(p == 2 * me + 1, 1.0, 0.0).astype(F32)
        a_send[t // 8, t % 8] = (cc16[0] * f0 + cc16[1] * f1).astype(BF16)
        return 0

    lax.fori_loop(0, 32, fill_a, 0)
    pl.semaphore_wait(barrier, count)

    a1 = {}
    for d in (1, 2, 3):
        a1[d] = go(
            send(
                a_send.at[(x + d) % 4], a_recv1.at[d], s_a1.at[d], r_a1.at[d], x_to[d], mp
            )
        )

    ids = [expert_ids[:, k : k + 1] for k in range(2)]
    gates = [gate_w[:, k : k + 1].astype(F32) for k in range(2)]
    lane8 = iota((SUF, 128), 1)
    onehot = (
        jnp.where(ids[0] == lane8, 1.0, 0.0) + jnp.where(ids[1] == lane8, 1.0, 0.0)
    ).astype(BF16)
    tri_r, tri_c = iota((SUF, SUF), 0), iota((SUF, SUF), 1)
    tri = jnp.where((tri_r // 4 == tri_c // 4) & (tri_c < tri_r), 1.0, 0.0).astype(BF16)
    before = jnp.dot(tri, onehot, preferred_element_type=F32)
    ranks = [
        jnp.sum(jnp.where(ids[k] == lane8, before, 0.0), axis=1, keepdims=True) for k in range(2)
    ]
    token = iota((SUF, 128), 0)
    lane = iota((SUF, 128), 1)
    place = (
        (token // 4 == (lane % 64) // 2)
        & (lane % 64 < 32)
        & (lane // 64 == me % 2)
    )
    lane_rank = (lane % 2).astype(F32)
    row16 = iota((16, 128), 0)

    def fill_g(e, _):
        total = jnp.zeros((1, 128), F32)
        for k in range(2):
            hit = place & (ids[k] == e) & (ranks[k] == lane_rank)
            total = total + jnp.sum(jnp.where(hit, gates[k], 0.0), axis=0, keepdims=True)
        gmat[e] = jnp.where(row16 == me // 2, jnp.broadcast_to(total, (16, 128)), 0.0).astype(BF16)
        return 0

    lax.fori_loop(0, EXPERTS, fill_g, 0)

    def fill_b(t, _):
        p = prefix_of[t]
        f0 = jnp.where(p == 2 * me, 1.0, 0.0).astype(F32)
        f1 = jnp.where(p == 2 * me + 1, 1.0, 0.0).astype(F32)
        b_send[t // 8, t % 8, :, 0:CH] = (ssm_cache[0] * f0 + ssm_cache[1] * f1).astype(BF16)
        b_send[t // 8, t % 8, :, CH : CH + 128] = gmat[t // 4]
        return 0

    lax.fori_loop(0, 32, fill_b, 0)

    for d in (1, 2, 3):
        a1[d].wait_recv()

    def mid_a(i, _):
        total = a_send[x, i].astype(F32)
        for d in (1, 2, 3):
            total = total + a_recv1[d, i].astype(F32)
        a_mid[i] = total.astype(BF16)
        return 0

    lax.fori_loop(0, 8, mid_a, 0)
    a2 = {}
    for d in range(1, 8):
        a2[d] = go(
            send(a_mid.at[(j + d) % 8], a_recv2.at[d], s_a2.at[d], r_a2.at[d], j_to[d], mp)
        )
    b1 = {}
    for d in (1, 2, 3):
        b1[d] = go(
            send(
                b_send.at[(x + d) % 4], b_recv1.at[d], s_b1.at[d], r_b1.at[d], x_to[d], mp
            )
        )

    def ow_id(px, pylo):
        return core * 16 + ((px + 4) % 4) * 4 + (pylo + 4) % 4

    oy = {}
    for d in (1, 2, 3):
        to = req_of(x, (ylo + d) % 4, core)
        oy[d] = go(send(out_w, ow.at[own_id], s_oy.at[d], r_oy.at[d], to, mp))
    ox = {}
    for way, d in ((0, 1), (1, 3)):
        ox[way, 0] = go(
            send(out_w, ow.at[own_id], s_ox.at[way, 0], r_ox.at[way, 0], x_to[d], mp)
        )
    os_ = {(0, 0): go(send(out_w, ow.at[own_id], s_os.at[0, 0], r_os.at[0, 0], sibling, mp))}

    xpad[8 : 8 + SUF, :] = xin[0].astype(F32)
    r4[...] = resid[...].astype(F32)
    for t in range(4):
        for q in range(8):
            r32[t * 8 + q : t * 8 + q + 1, :] = r4[t : t + 1, q * 512 : q * 512 + 512]
    d_send[:, :, 256:384] = jnp.zeros((8, 8, 128), F32)

    for d in range(1, 8):
        a2[d].wait_recv()
    total = a_mid[j].astype(F32)
    for d in range(1, 8):
        total = total + a_recv2[d].astype(F32)
    cs16[...] = total
    for k in range(3):
        for q in range(4):
            xpad[5 + k : 6 + k, q * 128 : q * 128 + 128] = cs16[4 * k + q : 4 * k + q + 1, :]

    conv = conv_w[0:1, :] * xpad[5 : 5 + SUF, :]
    for k in range(1, 4):
        conv = conv + conv_w[k : k + 1, :] * xpad[5 + k : 5 + k + SUF, :]
    conv = conv + conv_bias[...]
    u16 = silu(conv).astype(BF16)
    u_s[...] = u16.astype(F32)
    part = jnp.dot(u16, x_proj[:, 0:DTR], preferred_element_type=F32)
    part_bc = jnp.dot(u16, x_proj[:, DTR : DTR + 2 * NS], preferred_element_type=F32)
    d_send[:, :, 0:DTR] = part.reshape(8, 8, DTR)
    d_send[:, :, DTR : DTR + 2 * NS] = part_bc.reshape(8, 8, 2 * NS)

    d1 = {}
    for rel in mp_to:
        d1[rel] = go(
            send(
                d_send.at[(z + rel // 2) % 8],
                d_recv.at[rel],
                s_d1.at[rel],
                r_d1.at[rel],
                me,
                mp_to[rel],
            )
        )

    for d in (1, 2, 3):
        b1[d].wait_recv()

    def mid_b(i, _):
        total = b_send[x, i].astype(F32)
        for d in (1, 2, 3):
            total = total + b_recv1[d, i].astype(F32)
        b_mid[i] = total.astype(BF16)
        return 0

    lax.fori_loop(0, 8, mid_b, 0)
    b2 = {}
    for d in range(1, 8):
        b2[d] = go(
            send(b_mid.at[(j + d) % 8], b_recv2.at[d], s_b2.at[d], r_b2.at[d], j_to[d], mp)
        )

    for rel in mp_to:
        d1[rel].wait_recv()
    total = d_send[z]
    for rel in mp_to:
        total = total + d_recv[rel]
    d_sum[...] = total
    d_all[z] = total
    d2 = {}
    for dz in range(1, 8):
        d2[dz] = go(
            send(
                d_sum,
                d_all.at[z],
                s_d2.at[dz],
                r_d2.at[dz],
                me,
                ((z + dz) % 8) * 2 + hi,
            )
        )

    for d in (1, 2, 3):
        oy[d].wait_recv()
        block = ow.at[ow_id(x, ylo - d)]
        for way, dx in ((0, 1), (1, 3)):
            ox[way, d] = go(
                send(block, block, s_ox.at[way, d], r_ox.at[way, d], x_to[dx], mp)
            )
        os_[0, d] = go(send(block, block, s_os.at[0, d], r_os.at[0, d], sibling, mp))

    big_r, big_c = iota((512, 512), 0), iota((512, 512), 1)
    perm_big[...] = jnp.where(big_c == (big_r % 8) * 64 + big_r // 8, 1.0, 0.0).astype(BF16)
    small_r, small_c = iota((128, 128), 0), iota((128, 128), 1)
    perm_small[...] = jnp.where(small_c == (small_r % 16) * 8 + small_r // 16, 1.0, 0.0).astype(
        BF16
    )
    tok32 = iota((SUF, 32), 0)
    mine = tok32 == mp * 4 + iota((SUF, 32), 1) // 8
    sel_r, sel_c = iota((128, 32), 0), iota((128, 32), 1)
    chosen = jnp.zeros((128, 32), F32)
    for k in range(2):
        id_row = jnp.sum(jnp.where(mine, ids[k].astype(F32), 0.0), axis=0, keepdims=True)
        rank_row = jnp.sum(jnp.where(mine, ranks[k], 0.0), axis=0, keepdims=True)
        hit = (
            (sel_r % 8 == sel_c % 8)
            & ((sel_r // 16).astype(F32) == id_row)
            & (((sel_r // 8) % 2).astype(F32) == rank_row)
        )
        chosen = chosen + jnp.where(hit, 1.0, 0.0)
    sel[...] = chosen.astype(BF16)

    for dz in range(1, 8):
        d2[dz].wait_recv()
    dbc_in = d_all[:, :, 0:DTR].reshape(SUF, DTR).astype(BF16)
    pre = jnp.dot(dbc_in, dt_proj[...], preferred_element_type=F32) + dt_bias[...]
    dt_s[...] = jnp.maximum(pre, 0.0) + jnp.log1p(jnp.exp(-jnp.abs(pre)))
    mask_b = jnp.where(iota((NS, 128), 1) == iota((NS, 128), 0), 1.0, 0.0)
    mask_c = jnp.where(iota((NS, 128), 1) == iota((NS, 128), 0) + NS, 1.0, 0.0)

    def spread(i, _):
        rows = d_all[i, :, DTR : DTR + 128]
        for t in range(8):
            row = jnp.broadcast_to(rows[t : t + 1, :], (NS, 128))
            b_exp[i * 8 + t] = jnp.broadcast_to(
                jnp.sum(row * mask_b, axis=1, keepdims=True), (NS, 128)
            )
            c_exp[i * 8 + t] = jnp.broadcast_to(
                jnp.sum(row * mask_c, axis=1, keepdims=True), (NS, 128)
            )
        return 0

    lax.fori_loop(0, 8, spread, 0)

    for d in range(1, 8):
        b2[d].wait_recv()
    total = b_mid[j].astype(F32)
    for d in range(1, 8):
        total = total + b_recv2[d].astype(F32)
    gates16 = total[:, CH : CH + 128].astype(BF16)
    amat = -jnp.exp(a_log[...])

    def widen(v):
        return jnp.concatenate([v, v, v, v], axis=1)

    def scan8(i, state):
        dt8 = dt_s[pl.ds(pl.multiple_of(i * 8, 8), 8), :]
        u8 = u_s[pl.ds(pl.multiple_of(i * 8, 8), 8), :]
        du8 = dt8 * u8
        for t in range(8):
            decay = jnp.exp(dt8[t : t + 1, :] * amat)
            state = decay * state + widen(b_exp[i * 8 + t]) * du8[t : t + 1, :]
            yv_s[pl.ds(i * 8 + t, 1), :] = jnp.sum(
                widen(c_exp[i * 8 + t]) * state, axis=0, keepdims=True
            )
        return state

    state = lax.fori_loop(0, 8, scan8, total[:, 0:CH])
    state_out[...] = state

    ox2 = {}
    for k in range(4):
        for way, dx, back in ((0, 1, -1), (1, 3, 1)):
            ox[way, k].wait_recv()
            block = ow.at[ow_id(x + back, ylo - k)]
            if (k < 2) == (way == 0):
                ox2[k] = go(send(block, block, s_ox2.at[k], r_ox2.at[k], x_to[dx], mp))
            os_[1 + way, k] = go(
                send(block, block, s_os.at[1 + way, k], r_os.at[1 + way, k], sibling, mp)
            )

    gated = (yv_s[...] + d_skip[...] * u_s[...]) * silu(zin[0].astype(F32))
    ymix = gated.astype(BF16)

    for k in range(4):
        ox2[k].wait_recv()
        block = ow.at[ow_id(x + 2, ylo - k)]
        os_[3, k] = go(send(block, block, s_os.at[3, k], r_os.at[3, k], sibling, mp))
    load_o.wait()
    for key in os_:
        os_[key].wait_recv()

    def project(q, _):
        cols = jnp.concatenate(
            [ow[2 * q], ow[16 + 2 * q], ow[2 * q + 1], ow[17 + 2 * q]], axis=1
        )
        pq[pl.ds(pl.multiple_of(q * 64, 64), 64), :] = jnp.dot(
            ymix, cols, preferred_element_type=F32
        ).astype(BF16)
        return 0

    lax.fori_loop(0, 8, project, 0)

    def reorder(i, _):
        rows = jnp.dot(
            perm_big[pl.ds(pl.multiple_of(i * 128, 128), 128), :], pq[...], preferred_element_type=F32
        )
        p_send[pl.ds(i * 4, 4)] = rows.astype(BF16).reshape(4, 32, 512)
        return 0

    lax.fori_loop(0, 4, reorder, 0)
    ps = {}
    for rel in mp_to:
        ps[rel] = go(
            send(
                p_send.at[mp_to[rel]],
                p_recv.at[rel],
                s_p.at[rel],
                r_p.at[rel],
                me,
                mp_to[rel],
            )
        )
    hidden = r32[...] + p_send[mp].astype(F32)
    for rel in mp_to:
        ps[rel].wait_recv()
        hidden = hidden + p_recv[rel].astype(F32)

    for t in range(4):
        block = hidden[t * 8 : t * 8 + 8, :]
        square = jnp.sum(jnp.sum(block * block, axis=1, keepdims=True), axis=0, keepdims=True)
        scale = lax.rsqrt(square * (1.0 / D) + 1e-05)
        r32[t * 8 : t * 8 + 8, :] = block * scale * norm_gain[...]
        for q in range(8):
            h4[t : t + 1, q * 512 : q * 512 + 512] = block[q : q + 1, :]
    e_send[...] = (
        jnp.dot(sel[...], r32[...].astype(BF16), preferred_element_type=F32)
        .astype(BF16)
        .reshape(EXPERTS, 16, 512)
    )

    ex = {}
    for d in (1, 2, 3):
        ex[d] = go(
            send(
                e_send.at[pl.ds(2 * ((x + d) % 4), 2)],
                e_mid.at[:, x],
                s_ex.at[d],
                r_ex.at[d],
                x_to[d],
                mp,
            )
        )
    e_mid[0, x] = e_send[2 * x]
    e_mid[1, x] = e_send[2 * x + 1]
    stream_out[...] = h4[...].astype(BF16)
    load_g.wait()
    load_u.wait()
    for d in (1, 2, 3):
        ex[d].wait_recv()
    ey = {}
    for d in (7, 1, 6, 2, 5, 3, 4):
        parity = (((yy + d) % 8) % 4) // 2
        ey[d] = go(
            send(e_mid.at[parity], e_recv.at[d], s_ey.at[d], r_ey.at[d], y_to[d][0], y_to[d][1])
        )
    e_recv[0] = e_mid[ylo // 2]

    def ring(way, s, g):
        if way == 0:
            block, to = (z + 8 - (s - 1)) % 8, (z + 1) % 8
        else:
            block, to = (z + s - 1) % 8, (z + 7) % 8
        ref = xb.at[block, g, core]
        return go(
            send(ref, ref, s_zr.at[way, s, g], r_zr.at[way, s, g], me, to * 2 + hi)
        )

    def share(row, block, g):
        ref = xb.at[block, g, core]
        return go(send(ref, ref, s_zs.at[row, g], r_zs.at[row, g], sibling, mp))

    zr, zs = {}, {}
    for g in range(4):
        if g:
            ey[g].wait_recv()
        ey[7 - g].wait_recv()
        raw = jnp.concatenate(
            [e_recv[g].reshape(64, 512), e_recv[7 - g].reshape(64, 512)], axis=0
        )
        rows = jnp.dot(perm_small[...], raw, preferred_element_type=F32).astype(BF16)
        for q in range(8):
            xb[z, g, core, :, q * 512 : q * 512 + 512] = rows[q * 16 : q * 16 + 16, :]
        zr[0, 1, g] = ring(0, 1, g)
        zr[1, 1, g] = ring(1, 1, g)
        zs[0, g] = share(0, z, g)

    def expert(blocks):
        m = 128 * len(blocks)
        acc_g[0:m, :] = jnp.zeros((m, HID), F32)
        acc_u[0:m, :] = jnp.zeros((m, HID), F32)

        def tile(k, _):
            ks = pl.ds(pl.multiple_of(k * KT, KT), KT)
            left = jnp.concatenate([xb[b, :, :, :, ks].reshape(128, KT) for b in blocks], axis=0)
            acc_g[0:m, :] += jnp.dot(left, wg[ks, :], preferred_element_type=F32)
            acc_u[0:m, :] += jnp.dot(left, wu[ks, :], preferred_element_type=F32)
            return 0

        lax.fori_loop(0, D // KT, tile, 0)
        i_row = iota((128, 128), 0)
        i_lane = iota((128, 128), 1)
        grp, cc, yi, xs, kk = (
            i_row // 32,
            (i_row // 16) % 2,
            (i_row // 8) % 2,
            (i_row // 2) % 4,
            i_row % 2,
        )
        source = (yy + jnp.where(yi == 0, 8 - grp, grp + 1)) % 8
        pick = jnp.where(iota((128, 16), 1) == (xs * 4 + source % 4)[:, 0:16], 1.0, 0.0).astype(BF16)
        spread_g = jnp.dot(pick, gates16, preferred_element_type=F32)
        for n, b in enumerate(blocks):
            here = i_lane == cc * 64 + b * 4 + (source // 4) * 2 + kk
            weight = jnp.sum(jnp.where(here, spread_g, 0.0), axis=1, keepdims=True)
            rows = slice(n * 128, n * 128 + 128)
            act = silu(acc_g[rows, :]) * acc_u[rows, :] * weight
            for gi in range(4):
                for c in range(2):
                    for yi_ in range(2):
                        off = (8 - gi) % 8 if yi_ == 0 else gi + 1
                        at = gi * 32 + c * 16 + yi_ * 8
                        act_out[b, (yy + off) % 8, c] = act[at : at + 8, :]

    for s in range(1, 5):
        for g in range(4):
            if s <= steps_right(g):
                zr[0, s, g].wait_recv()
                if s + 1 <= steps_right(g):
                    zr[0, s + 1, g] = ring(0, s + 1, g)
                zs[2 * s - 1, g] = share(2 * s - 1, (z + 8 - s) % 8, g)
            if s <= steps_left(g):
                zr[1, s, g].wait_recv()
                if s + 1 <= steps_left(g):
                    zr[1, s + 1, g] = ring(1, s + 1, g)
                row = 2 * s if s < 4 else 7
                zs[row, g] = share(row, (z + s) % 8, g)
        if s == 1:
            for g in range(4):
                zs[0, g].wait_recv()
            expert([z])
        else:
            for g in range(4):
                zs[2 * s - 3, g].wait_recv()
                zs[2 * s - 2, g].wait_recv()
            expert([(z + 9 - s) % 8, (z + s - 1) % 8])
    for g in range(4):
        zs[7, g].wait_recv()
    expert([(z + 4) % 8])

    for copy in pending:
        copy.wait_send()


def local(
    xin,
    zin,
    conv_w,
    conv_bias,
    x_proj,
    dt_proj,
    dt_bias,
    a_log,
    d_skip,
    conv_cache,
    ssm_cache,
    prefix_of,
    out_w,
    resid,
    norm_gain,
    expert_ids,
    gate_w,
    w_gate,
    w_up,
):
    vmem = pl.BlockSpec(memory_space=pltpu.VMEM)
    smem = pl.BlockSpec(memory_space=pltpu.SMEM)
    hbm = pl.BlockSpec(memory_space=pl.ANY)
    dma = pltpu.SemaphoreType.DMA
    v = pltpu.VMEM
    scratch = [
        v((2, 16, 128), F32),
        v((16, 128), F32),
        v((72, CH), F32),
        v((4, 8, 16, 128), BF16),
        v((4, 8, 16, 128), BF16),
        v((8, 16, 128), BF16),
        v((8, 16, 128), BF16),
        v((4, 8, 16, CH + 128), BF16),
        v((4, 8, 16, CH + 128), BF16),
        v((8, 16, CH + 128), BF16),
        v((8, 16, CH + 128), BF16),
        v((8, 16, 128), BF16),
        v((8, 8, 384), F32),
        v((16, 8, 384), F32),
        v((8, 384), F32),
        v((8, 8, 384), F32),
        v((SUF, CH), F32),
        v((SUF, CH), F32),
        v((SUF, CH), F32),
        v((SUF, NS, 128), F32),
        v((SUF, NS, 128), F32),
        v((32, CH, 128), BF16),
        v((512, 512), BF16),
        v((512, 512), BF16),
        v((128, 128), BF16),
        v((16, 32, 512), BF16),
        v((16, 32, 512), BF16),
        v((4, D), F32),
        v((32, 512), F32),
        v((4, D), F32),
        v((128, 32), BF16),
        v((8, 16, 512), BF16),
        v((2, 4, 16, 512), BF16),
        v((8, 4, 16, 512), BF16),
        v((8, 4, 2, 16, D), BF16),
        v((D, HID), BF16),
        v((D, HID), BF16),
        v((256, HID), F32),
        v((256, HID), F32),
    ]
    sems = []
    for shape in (
        (4,),
        (8,),
        (4,),
        (8,),
        (16,),
        (8,),
        (4,),
        (2, 4),
        (4,),
        (4, 4),
        (16,),
        (4,),
        (8,),
        (2, 5, 4),
        (8, 4),
    ):
        sems += [dma(shape), dma(shape)]
    sems.append(dma((3,)))
    stream, state, act = pl.pallas_call(
        kernel,
        out_shape=(
            jax.ShapeDtypeStruct((4, D), BF16),
            jax.ShapeDtypeStruct((NS, CH), F32),
            jax.ShapeDtypeStruct((8, 8, 2, 8, HID), F32),
        ),
        in_specs=[smem] + [vmem] * 11 + [hbm] + [vmem] * 4 + [hbm] * 2,
        out_specs=(vmem, vmem, vmem),
        scratch_shapes=scratch + sems,
        compiler_params=pltpu.CompilerParams(
            collective_id=0, has_side_effects=True, vmem_limit_bytes=48 * 1024 * 1024
        ),
        name="mixer_and_experts",
    )(
        prefix_of,
        xin,
        zin,
        conv_w,
        conv_bias.reshape(1, CH),
        x_proj,
        dt_proj,
        dt_bias.reshape(1, CH),
        a_log,
        d_skip.reshape(1, CH),
        conv_cache,
        ssm_cache,
        out_w,
        resid,
        norm_gain.reshape(8, 512),
        expert_ids,
        gate_w,
        w_gate,
        w_up,
    )
    act = act.reshape(8, 2, 4, 2, 4, 2, HID).transpose(4, 2, 3, 0, 1, 5, 6)
    return (stream, state[None], act.astype(BF16).reshape(1, 1024, HID))


def solution(mesh):
    placed = (
        P("req", None, "mp"),
        P("req", None, "mp"),
        P(None, "mp"),
        P("mp"),
        P("mp", None),
        P(None, "mp"),
        P("mp"),
        P(None, "mp"),
        P("mp"),
        P("req", None, "mp"),
        P("req", None, "mp"),
        P(),
        P("mp", "req"),
        P(("req", "mp"), None),
        P(),
        P("req", None),
        P("req", None),
        P("req", None, "mp"),
        P("req", None, "mp"),
    )
    return jax.shard_map(
        local,
        mesh=mesh,
        in_specs=placed,
        out_specs=(P(("req", "mp"), None), P("req", None, "mp"), P("req", None, "mp")),
        check_vma=False,
    )
```

time: 765 us -> 156 us (0.20)
  waiting for transfers between devices: 506 us -> 0 us
  Pallas kernels: 0 us -> 134 us
  blocking collectives: 133 us -> 0 us
  other arithmetic: 59.5 us -> 0.07 us
  between operations: 18 us -> 0.69 us
  matrix products: 16.2 us -> 0 us
    unnamed x6 -> x0, waiting for transfers between devices: 194 us -> none
    psum x1 -> x0, waiting for transfers between devices: 183 us -> none  [local(): lax.psum(jnp.dot(u_act, x_proj, preferred_element_type=jnp.float32), 'mp')]
    pallas_call x0 -> x1, Pallas kernels: none -> 134 us  [local(): pl.pallas_call(kernel, out_shape=(jax.ShapeDtypeStruct((4, D), BF16), jax...]
    all_gather x3 -> x0, waiting for transfers between devices: 129 us -> none  [the longest x1 129 us: local(): pieces = lax.all_gather((got_x, got_g), 'mp', axis=1, tiled=True)]
    all_gather x2 -> x0, blocking collectives: 89.3 us -> none  [the longest x1 45.8 us: local(): lax.all_gather(conv_cache.astype(jnp.bfloat16), 'req', axis=0, tiled=True)]
    add x65 -> x0, other arithmetic: 44.5 us -> none  [the longest x64 44.5 us: advance(): out_now = jnp.sum(c_now[:, None] * state, axis=0) + d_skip * u_now]
    all_to_all x2 -> x0, blocking collectives: 43.5 us -> none  [the longest x1 32.9 us: local(): lax.all_to_all(send_x, 'req', split_axis=0, concat_axis=0, tiled=True)]
    dot_general x7 -> x0, matrix products: 16.2 us -> none  [the longest x1 5.86 us: expert_hidden(): gate_part = jnp.dot(flat, weight_gate, preferred_element_type=jnp.float32)]
  transfers between devices with their start and end apart: 5 -> 0, of which waited for: 3 -> 0; matrix products, arithmetic and copies ran while one was open for 8% -> 0% of each run, Pallas kernels for 0% -> 0%
where the time goes in v1:
time: 156 us; the launch traced here: 153 us
  Pallas kernels  134 us (86%)
  local copies, waits for them, and re-layouts  18 us (12%)
    pallas_call x1, Pallas kernels, local(): pl.pallas_call(kernel, out_shape=(jax.ShapeDtypeStruct((4, D), BF16), jax...  134 us
    unnamed x32, local copies, waits for them, and re-layouts  15.5 us

profile of v1, /device:TPU:1, one launch (start us, length us, event | category | flops | bytes accessed | tf_op | source)
XLA Modules:
  0.0 152.9 jit_solution(18288619303123144345)
XLA Ops:
  0.6 0.7 copy.23.conv_cache
  1.3 0.7 reshape.26.norm_gain
  2.1 0.8 copy.25.gate_w
  2.8 0.8 copy.24.expert_ids
  3.6 1.2 copy.22.x_proj
  4.8 1.6 %copy-done = bf16[1,4096,256]{2,1,0:T(8,128)(2,1)S(1)} copy-done((bf16[1,4096,256]{2,1,0:T(8,128)(2,1)S(1)}, bf16[1,4096,256]{2,1,0:T(8,128)(2,1)}, u32[]{:S(2)}) %copy-start) | copy-done | bytes 2097176
  6.4 0.9 copy-done.1
  7.3 0.9 copy-done.2
  8.2 0.8 copy-done.3
  9.1 0.8 copy-done.4
  9.9 0.8 copy-done.5
  10.7 0.8 copy-done.6
  11.5 0.8 copy-done.7
  12.3 0.7 copy-done.8
  13.0 0.7 copy-done.9
  13.6 0.7 copy-done.10
  14.3 0.7 copy-done.11
  15.0 0.7 copy-done.12
  15.7 134.1 %mixer_and_experts.1 = (bf16[4,4096]{1,0:T(4,128)(2,1)S(1)}, f32[16,512]{1,0:T(8,128)S(1)}, f32[8,8,2,8,256]{4,3,2,1,0:T(8,128)S(1)}) custom-call(s32[32]{0:T(128)S(1)} %copy-done.12, bf16[1,64,512]{2,1,0:T(8,128)(2,1)S(1)} %copy-done.3, bf16[1,64,512]{2,1,0:T(8,128)(2,1)S(1)} %copy-done.4, f32[4,512]{1,0:T(4,128)S(1)} %copy-done.8, f32[1,512]{1,0:T(1,128)S(1)} %bitcast.8, ...), custom_call_target="tpu_custom_call" | custom-call | tf_op jit(solution)/shard_map/mixer_and_experts/pallas_call | solution.py:742
  149.9 0.2 convert_element_type.10
  150.1 0.5 copy.26
  150.6 1.0 reshape.27
  151.6 0.6 copy.29
  152.2 0.6 copy.30
  (14 shorter events, 0.1 us)
Async XLA Ops:
  4.8 1.6 %copy-start = (bf16[1,4096,256]{2,1,0:T(8,128)(2,1)S(1)}, bf16[1,4096,256]{2,1,0:T(8,128)(2,1)}, u32[]{:S(2)}) copy-start(bf16[1,4096,256]{2,1,0:T(8,128)(2,1)} %w_gate.1) | copy-start | bytes 6291460
  6.4 0.9 copy-start.1
  7.3 0.9 copy-start.2
  8.2 0.8 copy-start.3
  9.1 0.8 copy-start.4
  9.9 0.8 copy-start.5
  10.7 0.8 copy-start.6
  11.5 0.8 copy-start.7
  12.3 0.7 copy-start.8
  13.0 0.7 copy-start.9
  13.6 0.7 copy-start.10
  14.3 0.7 copy-start.11
  15.0 0.7 copy-start.12

commit v2 on v0

v2 whole, which is shorter than its diff:
```python
import types

import jax
import jax.numpy as jnp
from jax import lax
from jax.experimental import pallas as pl
from jax.experimental.pallas import tpu as pltpu
from jax.sharding import PartitionSpec as P

F32 = jnp.float32
BF16 = jnp.bfloat16
MESH = pl.DeviceIdType.MESH

D = 4096
CH = 512
NS = 16
SUF = 64
DTR = 256
EXPERTS = 8
HID = 256
KT = 1024

VMEM = pltpu.VMEM
LOADED = {
    "prefix_of": pltpu.SMEM((32,), jnp.int32),
    "conv_cache": VMEM((3, 2, CH), F32),
    "ids": VMEM((2, SUF), jnp.int32),
    "gate_w": VMEM((2, SUF), BF16),
    "ssm_cache": VMEM((2, NS, CH), F32),
    "xin": VMEM((1, SUF, CH), BF16),
    "conv_w": VMEM((4, CH), F32),
    "conv_bias": VMEM((1, CH), F32),
    "x_proj": VMEM((DTR + 2 * NS, CH), BF16),
    "resid": VMEM((4, D), BF16),
    "norm_gain": VMEM((32, 128), F32),
    "dt_proj": VMEM((DTR, CH), BF16),
    "dt_bias": VMEM((1, CH), F32),
    "a_log": VMEM((NS, CH), F32),
    "d_skip": VMEM((1, CH), F32),
    "zin": VMEM((1, SUF, CH), BF16),
    "w_gate": VMEM((1, D, HID), BF16),
    "w_up": VMEM((1, D, HID), BF16),
}
SCRATCH = {
    "cc16": VMEM((2, 16, 128), F32),
    "cs16": VMEM((16, 128), F32),
    "xpad": VMEM((72, CH), F32),
    "a_send": VMEM((4, 8, 16, 128), BF16),
    "a_recv1": VMEM((4, 8, 16, 128), BF16),
    "a_mid": VMEM((8, 16, 128), BF16),
    "a_recv2": VMEM((8, 16, 128), BF16),
    "b_send": VMEM((4, 8, 16, CH + 128), BF16),
    "b_recv1": VMEM((4, 8, 16, CH + 128), BF16),
    "b_mid": VMEM((8, 16, CH + 128), BF16),
    "b_recv2": VMEM((8, 16, CH + 128), BF16),
    "gmat": VMEM((8, 16, 128), BF16),
    "d_send": VMEM((8, 8, 384), F32),
    "d_recv": VMEM((16, 8, 384), F32),
    "d_sum": VMEM((8, 384), F32),
    "d_all": VMEM((8, 8, 384), F32),
    "dt_s": VMEM((SUF, CH), F32),
    "u_s": VMEM((SUF, CH), F32),
    "yv_s": VMEM((SUF, CH), F32),
    "b_exp": VMEM((SUF, NS, 128), F32),
    "c_exp": VMEM((SUF, NS, 128), F32),
    "ow": VMEM((8, CH, 128), BF16),
    "ymix": VMEM((SUF, CH), BF16),
    "yfull": VMEM((4, SUF, CH), BF16),
    "perm_rows": VMEM((256, 256), BF16),
    "perm_small": VMEM((128, 128), BF16),
    "p_send": VMEM((16, 16, 1024), BF16),
    "p_recv": VMEM((16, 16, 1024), BF16),
    "p_sum": VMEM((16, 1024), F32),
    "hx_send": VMEM((4, 8, 512), F32),
    "hx_recv": VMEM((4, 8, 512), F32),
    "r4": VMEM((4, D), F32),
    "r32": VMEM((4, 8, 512), F32),
    "g8": VMEM((8, 512), F32),
    "g32": VMEM((4, 8, 512), F32),
    "n32": VMEM((32, 512), BF16),
    "h4": VMEM((4, D), F32),
    "sel": VMEM((128, 32), BF16),
    "e_send": VMEM((8, 16, 512), BF16),
    "e_mid": VMEM((2, 4, 16, 512), BF16),
    "e_recv": VMEM((3, 2, 4, 16, 512), BF16),
    "xb": VMEM((8, 4, 2, 16, D), BF16),
    "acc_g": VMEM((256, HID), F32),
    "acc_u": VMEM((256, HID), F32),
}
COPIES = {
    "a1": (4,),
    "a2": (8,),
    "b1": (4,),
    "b2": (8,),
    "d1": (16,),
    "d2": (8,),
    "oy": (4,),
    "os": (4,),
    "yx": (4,),
    "p": (16,),
    "hx": (4,),
    "ex": (4,),
    "ey": (6,),
    "zr": (2, 5, 3),
    "z4": (1,),
    "pr": (8,),
    "zs": (8, 4),
}
OPERANDS = list(LOADED) + ["out_w"]
BUFFERS = list(LOADED) + list(SCRATCH)


def iota(shape, dim):
    return lax.broadcasted_iota(jnp.int32, shape, dim)


def silu(v):
    return v / (1.0 + jnp.exp(-v))


def kernel(*refs):
    hbm = dict(zip(OPERANDS, refs))
    refs = refs[len(OPERANDS) :]
    stream_out, state_out, act_out = refs[:3]
    refs = refs[3:]
    b = types.SimpleNamespace(**dict(zip(BUFFERS, refs)))
    refs = refs[len(BUFFERS) :]
    sems = {name: (refs[2 * n], refs[2 * n + 1]) for n, name in enumerate(COPIES)}
    loc = refs[2 * len(COPIES)]

    me = lax.axis_index("req")
    mp = lax.axis_index("mp")
    x = me // 8
    ylo = (me // 2) % 4
    core = me % 2
    j = me % 8
    z = mp // 2
    hi = mp % 2
    yy = hi * 4 + ylo
    odd = ylo % 2
    pair = yy // 2

    def req_of(px, pylo, pcore):
        return px * 8 + pylo * 2 + pcore

    pending = []

    def send(name, at, src, dst, to_req, to_mp):
        copy = pltpu.make_async_remote_copy(
            src_ref=src,
            dst_ref=dst,
            send_sem=sems[name][0].at[at],
            recv_sem=sems[name][1].at[at],
            device_id=(to_req, to_mp),
            device_id_type=MESH,
        )
        copy.start()
        pending.append(copy)
        return copy

    loads = {}
    for n, name in enumerate(LOADED):
        loads[name] = pltpu.make_async_copy(hbm[name], getattr(b, name), loc.at[n])
        loads[name].start()
    load_o = pltpu.make_async_copy(hbm["out_w"], b.ow.at[j], loc.at[len(LOADED)])
    load_o.start()

    x_to = {d: req_of((x + d) % 4, ylo, core) for d in (1, 2, 3)}
    j_to = {d: x * 8 + (j + d) % 8 for d in range(1, 8)}
    mp_to = {}
    for dz in range(8):
        for dh in range(2):
            if dz or dh:
                mp_to[dz * 2 + dh] = ((z + dz) % 8) * 2 + (hi + dh) % 2
    sibling = req_of(x, ylo, 1 - core)
    partner = req_of(x, ylo + 1 - 2 * odd, core)

    barrier = pltpu.get_barrier_semaphore()
    greet = [(x_to[d], mp) for d in x_to]
    greet += [(j_to[d], mp) for d in j_to]
    greet += [(me, mp_to[d]) for d in mp_to]
    greet += [(req_of(x, (ylo + d) % 4, core), z * 2 + 1 - hi) for d in (1, 2, 3)]
    for to in greet:
        pl.semaphore_signal(barrier, inc=1, device_id=to, device_id_type=MESH)

    b.cc16[...] = jnp.zeros_like(b.cc16)
    loads["prefix_of"].wait()
    loads["conv_cache"].wait()
    for s in range(2):
        for k in range(3):
            for q in range(4):
                at = 4 * k + q
                b.cc16[s, at : at + 1, :] = b.conv_cache[k, s : s + 1, q * 128 : q * 128 + 128]

    def owned(t):
        p = b.prefix_of[t]
        f0 = jnp.where(p == 2 * me, 1.0, 0.0).astype(F32)
        f1 = jnp.where(p == 2 * me + 1, 1.0, 0.0).astype(F32)
        return f0, f1

    def fill_a(t, _):
        f0, f1 = owned(t)
        b.a_send[t // 8, t % 8] = (b.cc16[0] * f0 + b.cc16[1] * f1).astype(BF16)
        return 0

    lax.fori_loop(0, 32, fill_a, 0)
    pl.semaphore_wait(barrier, len(greet))

    a1 = {d: send("a1", d, b.a_send.at[(x + d) % 4], b.a_recv1.at[d], x_to[d], mp) for d in x_to}
    oy = {}
    for d in (1, 2, 3):
        to = req_of(x, (ylo + d) % 4, core)
        oy[d] = send("oy", d, hbm["out_w"], b.ow.at[j], to, mp)
    osib = {0: send("os", 0, hbm["out_w"], b.ow.at[j], sibling, mp)}

    loads["ids"].wait()
    loads["gate_w"].wait()
    eye = iota((SUF, SUF), 0) == iota((SUF, SUF), 1)

    def column(row):
        return jnp.sum(jnp.where(eye, row, 0.0), axis=1, keepdims=True)

    id_rows = b.ids[...].astype(F32)
    gate_rows = b.gate_w[...].astype(F32)
    ids = [column(id_rows[k : k + 1, :]) for k in range(2)]
    gates = [column(gate_rows[k : k + 1, :]) for k in range(2)]
    lane8 = iota((SUF, 128), 1).astype(F32)
    onehot = (
        jnp.where(ids[0] == lane8, 1.0, 0.0) + jnp.where(ids[1] == lane8, 1.0, 0.0)
    ).astype(BF16)
    tri_r, tri_c = iota((SUF, SUF), 0), iota((SUF, SUF), 1)
    tri = jnp.where((tri_r // 4 == tri_c // 4) & (tri_c < tri_r), 1.0, 0.0).astype(BF16)
    before = jnp.dot(tri, onehot, preferred_element_type=F32)
    ranks = [
        jnp.sum(jnp.where(ids[k] == lane8, before, 0.0), axis=1, keepdims=True) for k in range(2)
    ]
    lane = iota((1, 128), 1)
    lane_block = jnp.where((lane % 64 < 32) & (lane // 64 == core), (lane % 64) // 2, -1)
    place = iota((SUF, 1), 0) // 4 == lane_block
    lane_rank = (lane % 2).astype(F32)
    row16 = iota((16, 128), 0)

    def fill_g(e, _):
        total = jnp.zeros((1, 128), F32)
        for k in range(2):
            hit = place & (ids[k] == e.astype(F32)) & (ranks[k] == lane_rank)
            total = total + jnp.sum(jnp.where(hit, gates[k], 0.0), axis=0, keepdims=True)
        b.gmat[e] = jnp.where(row16 == me // 2, jnp.broadcast_to(total, (16, 128)), 0.0).astype(
            BF16
        )
        return 0

    lax.fori_loop(0, EXPERTS, fill_g, 0)
    loads["ssm_cache"].wait()

    def fill_b(t, _):
        f0, f1 = owned(t)
        b.b_send[t // 8, t % 8, :, 0:CH] = (b.ssm_cache[0] * f0 + b.ssm_cache[1] * f1).astype(BF16)
        b.b_send[t // 8, t % 8, :, CH : CH + 128] = b.gmat[t // 4]
        return 0

    lax.fori_loop(0, 32, fill_b, 0)

    for d in x_to:
        a1[d].wait_recv()

    def mid_a(i, _):
        total = b.a_send[x, i].astype(F32)
        for d in (1, 2, 3):
            total = total + b.a_recv1[d, i].astype(F32)
        b.a_mid[i] = total.astype(BF16)
        return 0

    lax.fori_loop(0, 8, mid_a, 0)
    a2 = {d: send("a2", d, b.a_mid.at[(j + d) % 8], b.a_recv2.at[d], j_to[d], mp) for d in j_to}
    b1 = {d: send("b1", d, b.b_send.at[(x + d) % 4], b.b_recv1.at[d], x_to[d], mp) for d in x_to}

    loads["xin"].wait()
    b.xpad[8 : 8 + SUF, :] = b.xin[0].astype(F32)
    b.d_send[:, :, 256:384] = jnp.zeros((8, 8, 128), F32)
    for name in ("conv_w", "conv_bias", "x_proj"):
        loads[name].wait()

    for d in j_to:
        a2[d].wait_recv()
    total = b.a_mid[j].astype(F32)
    for d in j_to:
        total = total + b.a_recv2[d].astype(F32)
    b.cs16[...] = total
    for k in range(3):
        for q in range(4):
            at = 4 * k + q
            b.xpad[5 + k : 6 + k, q * 128 : q * 128 + 128] = b.cs16[at : at + 1, :]

    conv = b.conv_w[0:1, :] * b.xpad[5 : 5 + SUF, :]
    for k in range(1, 4):
        conv = conv + b.conv_w[k : k + 1, :] * b.xpad[5 + k : 5 + k + SUF, :]
    conv = conv + b.conv_bias[...]
    u16 = silu(conv).astype(BF16)
    b.u_s[...] = u16.astype(F32)
    rows_by_rows = (((1,), (1,)), ((), ()))
    part = lax.dot_general(u16, b.x_proj[0:DTR, :], rows_by_rows, preferred_element_type=F32)
    part_bc = lax.dot_general(
        u16, b.x_proj[DTR : DTR + 2 * NS, :], rows_by_rows, preferred_element_type=F32
    )
    b.d_send[:, :, 0:DTR] = part.reshape(8, 8, DTR)
    b.d_send[:, :, DTR : DTR + 2 * NS] = part_bc.reshape(8, 8, 2 * NS)

    d1 = {
        rel: send("d1", rel, b.d_send.at[(z + rel // 2) % 8], b.d_recv.at[rel], me, mp_to[rel])
        for rel in mp_to
    }

    for d in x_to:
        b1[d].wait_recv()

    def mid_b(i, _):
        total = b.b_send[x, i].astype(F32)
        for d in (1, 2, 3):
            total = total + b.b_recv1[d, i].astype(F32)
        b.b_mid[i] = total.astype(BF16)
        return 0

    lax.fori_loop(0, 8, mid_b, 0)
    b2 = {d: send("b2", d, b.b_mid.at[(j + d) % 8], b.b_recv2.at[d], j_to[d], mp) for d in j_to}

    for rel in mp_to:
        d1[rel].wait_recv()
    total = b.d_send[z]
    for rel in mp_to:
        total = total + b.d_recv[rel]
    b.d_sum[...] = total
    b.d_all[z] = total
    d2 = {
        dz: send("d2", dz, b.d_sum, b.d_all.at[z], me, ((z + dz) % 8) * 2 + hi)
        for dz in range(1, 8)
    }

    for d in (1, 2, 3):
        oy[d].wait_recv()
        block = b.ow.at[((ylo + 4 - d) % 4) * 2 + core]
        osib[d] = send("os", d, block, block, sibling, mp)

    row = iota((256, 1), 0)
    target = ((row // 4) % 4) * 64 + (row // 16) * 4 + row % 4
    b.perm_rows[...] = jnp.where(iota((256, 256), 1) == target, 1.0, 0.0).astype(BF16)
    row = iota((128, 1), 0)
    target = (row % 16) * 8 + row // 16
    b.perm_small[...] = jnp.where(iota((128, 128), 1) == target, 1.0, 0.0).astype(BF16)
    col = iota((1, 32), 1)
    mine = iota((SUF, 1), 0) == mp * 4 + (col // 2) % 4
    col_group = (col // 8) * 2 + col % 2
    chosen = jnp.zeros((128, 32), F32)
    for k in range(2):
        id_row = jnp.sum(jnp.where(mine, ids[k], 0.0), axis=0, keepdims=True)
        rank_row = jnp.sum(jnp.where(mine, ranks[k], 0.0), axis=0, keepdims=True)
        hit = (
            (row % 8 == col_group)
            & ((row // 16).astype(F32) == id_row)
            & (((row // 8) % 2).astype(F32) == rank_row)
        )
        chosen = chosen + jnp.where(hit, 1.0, 0.0)
    b.sel[...] = chosen.astype(BF16)
    loads["resid"].wait()
    loads["norm_gain"].wait()
    b.r4[...] = b.resid[...].astype(F32)
    for q in range(8):
        for part_ in range(4):
            at = q * 4 + part_
            b.g8[q : q + 1, part_ * 128 : part_ * 128 + 128] = b.norm_gain[at : at + 1, :]
    for px in range(4):
        for t in range(4):
            for half in range(2):
                at, q = t * 2 + half, px * 2 + half
                b.r32[px, at : at + 1, :] = b.r4[t : t + 1, q * 512 : q * 512 + 512]
                b.g32[px, at : at + 1, :] = b.g8[q : q + 1, :]

    for name in ("dt_proj", "dt_bias", "a_log", "d_skip", "zin"):
        loads[name].wait()
    for dz in d2:
        d2[dz].wait_recv()
    dbc_in = b.d_all[:, :, 0:DTR].reshape(SUF, DTR).astype(BF16)
    pre = jnp.dot(dbc_in, b.dt_proj[...], preferred_element_type=F32) + b.dt_bias[...]
    b.dt_s[...] = jnp.maximum(pre, 0.0) + jnp.log1p(jnp.exp(-jnp.abs(pre)))
    mask_b = jnp.where(iota((NS, 128), 1) == iota((NS, 128), 0), 1.0, 0.0)
    mask_c = jnp.where(iota((NS, 128), 1) == iota((NS, 128), 0) + NS, 1.0, 0.0)

    def spread(i, _):
        rows = b.d_all[i, :, DTR : DTR + 128]
        for t in range(8):
            one = jnp.broadcast_to(rows[t : t + 1, :], (NS, 128))
            b.b_exp[i * 8 + t] = jnp.broadcast_to(
                jnp.sum(one * mask_b, axis=1, keepdims=True), (NS, 128)
            )
            b.c_exp[i * 8 + t] = jnp.broadcast_to(
                jnp.sum(one * mask_c, axis=1, keepdims=True), (NS, 128)
            )
        return 0

    lax.fori_loop(0, 8, spread, 0)

    for d in j_to:
        b2[d].wait_recv()
    total = b.b_mid[j].astype(F32)
    for d in j_to:
        total = total + b.b_recv2[d].astype(F32)
    gates16 = total[:, CH : CH + 128].astype(BF16)
    amat = -jnp.exp(b.a_log[...])

    def widen(v):
        return jnp.concatenate([v, v, v, v], axis=1)

    def scan8(i, state):
        at = pl.ds(pl.multiple_of(i * 8, 8), 8)
        dt8 = b.dt_s[at, :]
        du8 = dt8 * b.u_s[at, :]
        for t in range(8):
            decay = jnp.exp(dt8[t : t + 1, :] * amat)
            state = decay * state + widen(b.b_exp[i * 8 + t]) * du8[t : t + 1, :]
            b.yv_s[pl.ds(i * 8 + t, 1), :] = jnp.sum(
                widen(b.c_exp[i * 8 + t]) * state, axis=0, keepdims=True
            )
        return state

    state = lax.fori_loop(0, 8, scan8, total[:, 0:CH])
    gated = (b.yv_s[...] + b.d_skip[...] * b.u_s[...]) * silu(b.zin[0].astype(F32))
    ymix = gated.astype(BF16)
    b.ymix[...] = ymix
    b.yfull[x] = ymix

    yx = {d: send("yx", d, b.ymix, b.yfull.at[x], x_to[d], mp) for d in x_to}
    state_out[...] = state
    load_o.wait()
    for d in osib:
        osib[d].wait_recv()
    for d in x_to:
        yx[d].wait_recv()
    left = jnp.dot(
        b.perm_rows[...], b.yfull[...].reshape(256, CH), preferred_element_type=F32
    ).astype(BF16)
    for n in range(4):
        cols = jnp.concatenate([b.ow[2 * n], b.ow[2 * n + 1]], axis=1)
        part = jnp.dot(left, cols, preferred_element_type=F32).astype(BF16)
        b.p_send[:, :, n * 256 : n * 256 + 256] = part.reshape(16, 16, 256)
    ps = {
        rel: send("p", rel, b.p_send.at[mp_to[rel]], b.p_recv.at[rel], me, mp_to[rel])
        for rel in mp_to
    }
    total = b.p_send[mp].astype(F32)
    for rel in mp_to:
        ps[rel].wait_recv()
        total = total + b.p_recv[rel].astype(F32)
    b.p_sum[...] = total
    for px in range(4):
        for t in range(4):
            for half in range(2):
                at = t * 2 + half
                b.hx_send[px, at : at + 1, :] = b.p_sum[
                    px * 4 + t : px * 4 + t + 1, half * 512 : half * 512 + 512
                ]
    hx = {d: send("hx", d, b.hx_send.at[(x + d) % 4], b.hx_recv.at[x], x_to[d], mp) for d in x_to}
    b.hx_recv[x] = b.hx_send[x]
    for d in x_to:
        hx[d].wait_recv()

    hidden = [b.hx_recv[px] + b.r32[px] for px in range(4)]
    square = hidden[0] * hidden[0]
    for px in range(1, 4):
        square = square + hidden[px] * hidden[px]
    square = jnp.sum(square, axis=1, keepdims=True)
    scales = []
    for t in range(4):
        mean = (square[2 * t : 2 * t + 1] + square[2 * t + 1 : 2 * t + 2]) * (1.0 / D)
        scales += [lax.rsqrt(mean + 1e-05)] * 2
    scale = jnp.concatenate([jnp.broadcast_to(v, (1, 512)) for v in scales], axis=0)
    normed = [hidden[px] * scale * b.g32[px] for px in range(4)]
    b.n32[...] = jnp.concatenate(normed, axis=0).astype(BF16)
    b.e_send[...] = (
        jnp.dot(b.sel[...], b.n32[...], preferred_element_type=F32)
        .astype(BF16)
        .reshape(EXPERTS, 16, 512)
    )

    ex = {
        d: send(
            "ex", d, b.e_send.at[pl.ds(2 * ((x + d) % 4), 2)], b.e_mid.at[:, x], x_to[d], mp
        )
        for d in x_to
    }
    b.e_mid[0, x] = b.e_send[2 * x]
    b.e_mid[1, x] = b.e_send[2 * x + 1]
    for px in range(4):
        for t in range(4):
            for half in range(2):
                at, q = t * 2 + half, px * 2 + half
                b.h4[t : t + 1, q * 512 : q * 512 + 512] = hidden[px][at : at + 1, :]
    stream_out[...] = b.h4[...].astype(BF16)
    for d in x_to:
        ex[d].wait_recv()

    kind = pair % 2

    def send_y(slot, to_y, parity):
        return send(
            "ey",
            slot * 2 + odd,
            b.e_mid.at[parity],
            b.e_recv.at[slot, odd],
            req_of(x, to_y % 4, core),
            z * 2 + to_y // 4,
        )

    send_y(0, yy + 1 - 2 * odd, kind)
    send_y(1, 2 * ((pair + 1) % 4), 1 - kind)
    send_y(1, 2 * ((pair + 3) % 4) + 1, 1 - kind)
    send_y(2, 2 * ((pair + 2) % 4), kind)
    send_y(2, 2 * ((pair + 2) % 4) + 1, kind)
    b.e_recv[0, odd] = b.e_mid[kind]

    def got_y(slot, member):
        pltpu.make_async_remote_copy(
            src_ref=b.e_mid.at[0],
            dst_ref=b.e_recv.at[slot, member],
            send_sem=sems["ey"][0].at[slot * 2 + member],
            recv_sem=sems["ey"][1].at[slot * 2 + member],
            device_id=(me, mp),
            device_id_type=MESH,
        ).wait_recv()

    own_side = 3 - 2 * odd
    chunk = (0, own_side, 2)

    def ring(way, s, i):
        if way == 0:
            block, to = (z + 8 - (s - 1)) % 8, (z + 1) % 8
        else:
            block, to = (z + s - 1) % 8, (z + 7) % 8
        ref = b.xb.at[block, chunk[i], core]
        return send("zr", (way, s, i), ref, ref, me, to * 2 + hi)

    def in_ring(way, s, i):
        return s <= 3 or (s == 4 and i == way)

    def share(row, block, i):
        ref = b.xb.at[block, chunk[i] if i < 3 else 4 - own_side, core]
        return send("zs", (row, i), ref, ref, sibling, mp)

    def to_pair(row, block):
        ref = b.xb.at[block, own_side, core]
        return send("pr", row, ref, ref, partner, mp)

    block_of = {0: z, 7: (z + 4) % 8}
    for s in (1, 2, 3):
        block_of[2 * s - 1] = (z + 8 - s) % 8
        block_of[2 * s] = (z + s) % 8

    zr, zs, pr = {}, {}, {}
    for i in range(3):
        if i == 0:
            got_y(0, 1 - odd)
        else:
            got_y(i, 0)
            got_y(i, 1)
        raw = b.e_recv[i].reshape(128, 512)
        rows = jnp.dot(b.perm_small[...], raw, preferred_element_type=F32).astype(BF16)
        for q in range(8):
            b.xb[z, chunk[i], core, :, q * 512 : q * 512 + 512] = rows[q * 16 : q * 16 + 16, :]
        zr[0, 1, i] = ring(0, 1, i)
        zr[1, 1, i] = ring(1, 1, i)
        zs[0, i] = share(0, z, i)
        if i == 1:
            pr[0] = to_pair(0, z)

    def handle(s, i):
        for way in (0, 1):
            if (way, s, i) not in zr:
                continue
            zr[way, s, i].wait_recv()
            if in_ring(way, s + 1, i):
                zr[way, s + 1, i] = ring(way, s + 1, i)
            row = 2 * s - 1 + way if s < 4 else 7
            zs[row, i] = share(row, block_of[row], i)
            if i == 1:
                pr[row] = to_pair(row, block_of[row])

    def from_pair(rows):
        for row in rows:
            pr[row].wait_recv()
            zs[row, 3] = share(row, block_of[row], 3)

    i_row = iota((128, 1), 0)
    grp, cc, yi, xs, kk = (
        i_row // 32,
        (i_row // 16) % 2,
        (i_row // 8) % 2,
        (i_row // 2) % 4,
        i_row % 2,
    )
    source = (2 * pair + 2 * grp + yi) % 8
    pick = jnp.where(iota((128, 16), 1) == xs * 4 + source % 4, 1.0, 0.0).astype(BF16)
    spread_g = jnp.dot(pick, gates16, preferred_element_type=F32)
    gate_lane = cc * 64 + (source // 4) * 2 + kk

    def expert(rows):
        for row in rows:
            for i in range(4):
                zs[row, i].wait_recv()
        blocks = [block_of[row] for row in rows]
        m = 128 * len(blocks)
        b.acc_g[0:m, :] = jnp.zeros((m, HID), F32)
        b.acc_u[0:m, :] = jnp.zeros((m, HID), F32)

        def tile(k, _):
            ks = pl.ds(pl.multiple_of(k * KT, KT), KT)
            slots = jnp.concatenate(
                [b.xb[block, :, :, :, ks].reshape(128, KT) for block in blocks], axis=0
            )
            b.acc_g[0:m, :] += jnp.dot(slots, b.w_gate[0, ks, :], preferred_element_type=F32)
            b.acc_u[0:m, :] += jnp.dot(slots, b.w_up[0, ks, :], preferred_element_type=F32)
            return 0

        lax.fori_loop(0, D // KT, tile, 0)
        for n, block in enumerate(blocks):
            here = iota((128, 128), 1) == gate_lane + block * 4
            weight = jnp.sum(jnp.where(here, spread_g, 0.0), axis=1, keepdims=True)
            part = slice(n * 128, n * 128 + 128)
            act = silu(b.acc_g[part, :]) * b.acc_u[part, :] * weight
            for g in range(4):
                for c in range(2):
                    for member in range(2):
                        at = g * 32 + c * 16 + member * 8
                        act_out[block, (2 * pair + 2 * g + member) % 8, c] = act[at : at + 8, :]

    loads["w_gate"].wait()
    loads["w_up"].wait()
    for s in (1, 2, 3):
        for i in range(3):
            handle(s, i)
        if s == 3:
            ref = b.xb.at[(z + 5 + core * 6) % 8, 2, core]
            z4 = send("z4", 0, ref, ref, me, ((z + 1 + core * 6) % 8) * 2 + hi)
        from_pair([0] if s == 1 else [2 * s - 3, 2 * s - 2])
        if s == 2:
            expert([0])
        if s == 3:
            expert([1, 2])
    handle(4, 0)
    handle(4, 1)
    from_pair([5, 6])
    expert([3, 4])
    z4.wait_recv()
    zs[7, 2] = share(7, block_of[7], 2)
    expert([5, 6])
    from_pair([7])
    expert([7])

    for copy in pending:
        copy.wait_send()


def local(
    xin,
    zin,
    conv_w,
    conv_bias,
    x_proj,
    dt_proj,
    dt_bias,
    a_log,
    d_skip,
    conv_cache,
    ssm_cache,
    prefix_of,
    out_w,
    resid,
    norm_gain,
    expert_ids,
    gate_w,
    w_gate,
    w_up,
):
    operands = {
        "prefix_of": prefix_of,
        "conv_cache": conv_cache.transpose(1, 0, 2),
        "ids": expert_ids.T,
        "gate_w": gate_w.T,
        "ssm_cache": ssm_cache,
        "xin": xin,
        "conv_w": conv_w,
        "conv_bias": conv_bias.reshape(1, CH),
        "x_proj": x_proj.T,
        "resid": resid,
        "norm_gain": norm_gain.reshape(32, 128),
        "dt_proj": dt_proj,
        "dt_bias": dt_bias.reshape(1, CH),
        "a_log": a_log,
        "d_skip": d_skip.reshape(1, CH),
        "zin": zin,
        "w_gate": w_gate,
        "w_up": w_up,
        "out_w": out_w,
    }
    vmem = pl.BlockSpec(memory_space=VMEM)
    dma = pltpu.SemaphoreType.DMA
    sems = []
    for shape in COPIES.values():
        sems += [dma(shape), dma(shape)]
    sems.append(dma((len(LOADED) + 1,)))
    stream, state, act = pl.pallas_call(
        kernel,
        out_shape=(
            jax.ShapeDtypeStruct((4, D), BF16),
            jax.ShapeDtypeStruct((NS, CH), F32),
            jax.ShapeDtypeStruct((8, 8, 2, 8, HID), F32),
        ),
        in_specs=[pl.BlockSpec(memory_space=pltpu.HBM)] * len(OPERANDS),
        out_specs=(vmem, vmem, vmem),
        scratch_shapes=list(LOADED.values()) + list(SCRATCH.values()) + sems,
        compiler_params=pltpu.CompilerParams(
            collective_id=0, has_side_effects=True, vmem_limit_bytes=60 * 1024 * 1024
        ),
        name="mixer_and_experts",
    )(*[operands[name] for name in OPERANDS])
    act = act.reshape(8, 2, 4, 2, 4, 2, HID).transpose(4, 2, 3, 0, 1, 5, 6)
    return (stream, state[None], act.astype(BF16).reshape(1, 1024, HID))


def solution(mesh):
    placed = (
        P("req", None, "mp"),
        P("req", None, "mp"),
        P(None, "mp"),
        P("mp"),
        P("mp", None),
        P(None, "mp"),
        P("mp"),
        P(None, "mp"),
        P("mp"),
        P("req", None, "mp"),
        P("req", None, "mp"),
        P(),
        P("mp", "req"),
        P(("req", "mp"), None),
        P(),
        P("req", None),
        P("req", None),
        P("req", None, "mp"),
        P("req", None, "mp"),
    )
    return jax.shard_map(
        local,
        mesh=mesh,
        in_specs=placed,
        out_specs=(P(("req", "mp"), None), P("req", None, "mp"), P("req", None, "mp")),
        check_vma=False,
    )
```

time: 765 us -> 127 us (0.17)
  waiting for transfers between devices: 506 us -> 0 us
  blocking collectives: 133 us -> 0 us
  Pallas kernels: 0 us -> 122 us
  other arithmetic: 59.5 us -> 1.3 us
  local copies, waits for them, and re-layouts: 23.4 us -> 2.97 us
  between operations: 18 us -> 0.68 us
  matrix products: 16.2 us -> 0 us
    unnamed x6 -> x0, waiting for transfers between devices: 194 us -> none
    psum x1 -> x0, waiting for transfers between devices: 183 us -> none  [local(): lax.psum(jnp.dot(u_act, x_proj, preferred_element_type=jnp.float32), 'mp')]
    all_gather x3 -> x0, waiting for transfers between devices: 129 us -> none  [the longest x1 129 us: local(): pieces = lax.all_gather((got_x, got_g), 'mp', axis=1, tiled=True)]
    pallas_call x0 -> x1, Pallas kernels: none -> 122 us  [local(): pl.pallas_call(kernel, out_shape=(jax.ShapeDtypeStruct((4, D), BF16), jax...]
    all_gather x2 -> x0, blocking collectives: 89.3 us -> none  [the longest x1 45.8 us: local(): lax.all_gather(conv_cache.astype(jnp.bfloat16), 'req', axis=0, tiled=True)]
    add x65 -> x0, other arithmetic: 44.5 us -> none  [the longest x64 44.5 us: advance(): out_now = jnp.sum(c_now[:, None] * state, axis=0) + d_skip * u_now]
    all_to_all x2 -> x0, blocking collectives: 43.5 us -> none  [the longest x1 32.9 us: local(): lax.all_to_all(send_x, 'req', split_axis=0, concat_axis=0, tiled=True)]
    dot_general x7 -> x0, matrix products: 16.2 us -> none  [the longest x1 5.86 us: expert_hidden(): gate_part = jnp.dot(flat, weight_gate, preferred_element_type=jnp.float32)]
  transfers between devices with their start and end apart: 5 -> 0, of which waited for: 3 -> 0; matrix products, arithmetic and copies ran while one was open for 8% -> 0% of each run, Pallas kernels for 0% -> 0%
where the time goes in v2:
time: 127 us
  Pallas kernels  122 us (96%)
  local copies, waits for them, and re-layouts  2.97 us (2%)
  other arithmetic  1.3 us (1%)
    pallas_call x1, Pallas kernels, local(): pl.pallas_call(kernel, out_shape=(jax.ShapeDtypeStruct((4, D), BF16), jax...  122 us

profile of v2, /device:TPU:1, one launch (start us, length us, event | category | flops | bytes accessed | tf_op | source)
XLA Modules:
  0.0 126.8 jit_solution(14015898057597589898)
XLA Ops:
  0.6 121.9 %mixer_and_experts.1 = (bf16[4,4096]{1,0:T(4,128)(2,1)}, f32[16,512]{1,0:T(8,128)}, f32[8,8,2,8,256]{4,3,2,1,0:T(8,128)}) custom-call(s32[32]{0:T(128)} %refs_0_.1, f32[3,2,512]{2,1,0:T(2,128)} %bitcast.16, s32[2,64]{1,0:T(2,128)} %bitcast.20, bf16[2,64]{1,0:T(2,128)(2,1)} %bitcast.21, f32[2,16,512]{2,1,0:T(8,128)} %refs_4_.1, bf16[1,64,512]{2,1,0:T(8,128)(2,1)} %refs_5_.1, ...), custom_call_target="tpu_custom_call" | custom-call | tf_op jit(solution)/shard_map/mixer_and_experts/pallas_call | solution.py:709
  122.5 0.0 copy-start.1
  122.5 0.0 copy-start
  122.5 1.3 %convert_element_type.9 = bf16[8,8,2,8,256]{4,3,2,1,0:T(8,128)(2,1)S(1)} convert(f32[8,8,2,8,256]{4,3,2,1,0:T(8,128)} %get-tuple-element.8) | non-fusion elementwise | flops 262144 | bytes 1572864 | tf_op jit(solution)/shard_map/convert_element_type | solution.py:725
  123.8 0.2 convert_element_type.10
  124.0 0.5 copy.22
  124.6 1.0 reshape.27
  125.6 0.0 copy-done.1
  125.6 0.6 copy.25
  126.2 0.0 copy-done
  126.2 0.6 copy.26
Async XLA Ops:
  122.5 3.1 %copy-start.1 = (bf16[4,4096]{1,0:T(4,128)(2,1)S(1)}, bf16[4,4096]{1,0:T(4,128)(2,1)}, u32[]{:S(2)}) copy-start(bf16[4,4096]{1,0:T(4,128)(2,1)} %get-tuple-element.12) | copy-start | bytes 98308
  122.5 3.7 %copy-start = (f32[16,512]{1,0:T(8,128)S(1)}, f32[16,512]{1,0:T(8,128)}, u32[]{:S(2)}) copy-start(f32[16,512]{1,0:T(8,128)} %get-tuple-element.7) | copy-start | bytes 98308

commit v3 on v2

--- a/solution.py
+++ b/solution.py
@@ -58,15 +58,18 @@
     "d_recv": VMEM((16, 8, 384), F32),
     "d_sum": VMEM((8, 384), F32),
     "d_all": VMEM((8, 8, 384), F32),
+    "l_send": VMEM((8, 128), F32),
+    "l_recv": VMEM((16, 8, 128), F32),
     "dt_s": VMEM((SUF, CH), F32),
     "u_s": VMEM((SUF, CH), F32),
     "yv_s": VMEM((SUF, CH), F32),
     "b_exp": VMEM((SUF, NS, 128), F32),
     "c_exp": VMEM((SUF, NS, 128), F32),
     "ow": VMEM((8, CH, 128), BF16),
-    "ymix": VMEM((SUF, CH), BF16),
-    "yfull": VMEM((4, SUF, CH), BF16),
-    "perm_rows": VMEM((256, 256), BF16),
+    "ymix": VMEM((2, 32, CH), BF16),
+    "yfull": VMEM((2, 4, 32, CH), BF16),
+    "perm_rows": VMEM((128, 128), BF16),
+    "perm_out": VMEM((128, 128), BF16),
     "perm_small": VMEM((128, 128), BF16),
     "p_send": VMEM((16, 16, 1024), BF16),
     "p_recv": VMEM((16, 16, 1024), BF16),
@@ -86,6 +89,7 @@
     "xb": VMEM((8, 4, 2, 16, D), BF16),
     "acc_g": VMEM((256, HID), F32),
     "acc_u": VMEM((256, HID), F32),
+    "act_s": VMEM((8, 8, 2, 8, HID), F32),
 }
 COPIES = {
     "a1": (4,),
@@ -94,9 +98,10 @@
     "b2": (8,),
     "d1": (16,),
     "d2": (8,),
+    "l1": (16,),
     "oy": (4,),
     "os": (4,),
-    "yx": (4,),
+    "yx": (2, 4),
     "p": (16,),
     "hx": (4,),
     "ex": (4,),
@@ -110,6 +115,10 @@
 BUFFERS = list(LOADED) + list(SCRATCH)
 
 
+def mod(a, n):
+    return lax.rem(a, jnp.int32(n))
+
+
 def iota(shape, dim):
     return lax.broadcasted_iota(jnp.int32, shape, dim)
 
@@ -130,15 +139,16 @@
 
     me = lax.axis_index("req")
     mp = lax.axis_index("mp")
-    x = me // 8
-    ylo = (me // 2) % 4
-    core = me % 2
-    j = me % 8
-    z = mp // 2
-    hi = mp % 2
+    x = lax.div(me, jnp.int32(8))
+    j = mod(me, 8)
+    ylo = lax.div(j, jnp.int32(2))
+    core = mod(me, 2)
+    z = lax.div(mp, jnp.int32(2))
+    hi = mod(mp, 2)
     yy = hi * 4 + ylo
-    odd = ylo % 2
-    pair = yy // 2
+    odd = mod(ylo, 2)
+    pair = lax.div(yy, jnp.int32(2))
+    half_of = lax.div(z, jnp.int32(4))
 
     def req_of(px, pylo, pcore):
         return px * 8 + pylo * 2 + pcore
@@ -165,13 +175,15 @@
     load_o = pltpu.make_async_copy(hbm["out_w"], b.ow.at[j], loc.at[len(LOADED)])
     load_o.start()
 
-    x_to = {d: req_of((x + d) % 4, ylo, core) for d in (1, 2, 3)}
-    j_to = {d: x * 8 + (j + d) % 8 for d in range(1, 8)}
+    x_at = {d: mod(x + d, 4) for d in (1, 2, 3)}
+    j_at = {d: mod(j + d, 8) for d in range(1, 8)}
+    x_to = {d: req_of(x_at[d], ylo, core) for d in (1, 2, 3)}
+    j_to = {d: x * 8 + j_at[d] for d in range(1, 8)}
     mp_to = {}
     for dz in range(8):
         for dh in range(2):
             if dz or dh:
-                mp_to[dz * 2 + dh] = ((z + dz) % 8) * 2 + (hi + dh) % 2
+                mp_to[dz * 2 + dh] = mod(z + dz, 8) * 2 + mod(hi + dh, 2)
     sibling = req_of(x, ylo, 1 - core)
     partner = req_of(x, ylo + 1 - 2 * odd, core)
 
@@ -179,7 +191,7 @@
     greet = [(x_to[d], mp) for d in x_to]
     greet += [(j_to[d], mp) for d in j_to]
     greet += [(me, mp_to[d]) for d in mp_to]
-    greet += [(req_of(x, (ylo + d) % 4, core), z * 2 + 1 - hi) for d in (1, 2, 3)]
+    greet += [(req_of(x, mod(ylo + d, 4), core), z * 2 + 1 - hi) for d in (1, 2, 3)]
     for to in greet:
         pl.semaphore_signal(barrier, inc=1, device_id=to, device_id_type=MESH)
 
@@ -206,10 +218,51 @@
     lax.fori_loop(0, 32, fill_a, 0)
     pl.semaphore_wait(barrier, len(greet))
 
-    a1 = {d: send("a1", d, b.a_send.at[(x + d) % 4], b.a_recv1.at[d], x_to[d], mp) for d in x_to}
+    a1 = {d: send("a1", d, b.a_send.at[x_at[d]], b.a_recv1.at[d], x_to[d], mp) for d in x_to}
+
+    loads["xin"].wait()
+    b.xpad[0:8, :] = jnp.zeros((8, CH), F32)
+    b.xpad[8 : 8 + SUF, :] = b.xin[0].astype(F32)
+    b.d_send[:, :, 256:384] = jnp.zeros((8, 8, 128), F32)
+    for name in ("conv_w", "conv_bias", "x_proj"):
+        loads[name].wait()
+    rows_by_rows = (((1,), (1,)), ((), ()))
+
+    def project_in(n):
+        conv = b.conv_w[0:1, :] * b.xpad[5 : 5 + n, :]
+        for k in range(1, 4):
+            conv = conv + b.conv_w[k : k + 1, :] * b.xpad[5 + k : 5 + k + n, :]
+        u16 = silu(conv + b.conv_bias[...]).astype(BF16)
+        b.u_s[0:n, :] = u16.astype(F32)
+        part = lax.dot_general(u16, b.x_proj[0:DTR, :], rows_by_rows, preferred_element_type=F32)
+        part_bc = lax.dot_general(
+            u16, b.x_proj[DTR : DTR + 2 * NS, :], rows_by_rows, preferred_element_type=F32
+        )
+        b.d_send[0 : n // 8, :, 0:DTR] = part.reshape(n // 8, 8, DTR)
+        b.d_send[0 : n // 8, :, DTR : DTR + 2 * NS] = part_bc.reshape(n // 8, 8, 2 * NS)
+
+    project_in(SUF)
+    d1 = {
+        rel: send("d1", rel, b.d_send.at[mod(z + rel // 2, 8)], b.d_recv.at[rel], me, mp_to[rel])
+        for rel in mp_to
+    }
+
+    for d in x_to:
+        a1[d].wait_recv()
+
+    def mid_a(i, _):
+        total = b.a_send[x, i].astype(F32)
+        for d in (1, 2, 3):
+            total = total + b.a_recv1[d, i].astype(F32)
+        b.a_mid[i] = total.astype(BF16)
+        return 0
+
+    lax.fori_loop(0, 8, mid_a, 0)
+    a2 = {d: send("a2", d, b.a_mid.at[j_at[d]], b.a_recv2.at[d], j_to[d], mp) for d in j_to}
+
     oy = {}
     for d in (1, 2, 3):
-        to = req_of(x, (ylo + d) % 4, core)
+        to = req_of(x, mod(ylo + d, 4), core)
         oy[d] = send("oy", d, hbm["out_w"], b.ow.at[j], to, mp)
     osib = {0: send("os", 0, hbm["out_w"], b.ow.at[j], sibling, mp)}
 
@@ -228,7 +281,7 @@
     onehot = (
         jnp.where(ids[0] == lane8, 1.0, 0.0) + jnp.where(ids[1] == lane8, 1.0, 0.0)
     ).astype(BF16)
-    tri_r, tri_c = iota((SUF, SUF), 0), iota((SUF, SUF), 1)
+    tri_r, tri_c = iota((SUF, 1), 0), iota((1, SUF), 1)
     tri = jnp.where((tri_r // 4 == tri_c // 4) & (tri_c < tri_r), 1.0, 0.0).astype(BF16)
     before = jnp.dot(tri, onehot, preferred_element_type=F32)
     ranks = [
@@ -245,41 +298,24 @@
         for k in range(2):
             hit = place & (ids[k] == e.astype(F32)) & (ranks[k] == lane_rank)
             total = total + jnp.sum(jnp.where(hit, gates[k], 0.0), axis=0, keepdims=True)
-        b.gmat[e] = jnp.where(row16 == me // 2, jnp.broadcast_to(total, (16, 128)), 0.0).astype(
-            BF16
-        )
+        b.gmat[e] = jnp.where(
+            row16 == lax.div(me, jnp.int32(2)), jnp.broadcast_to(total, (16, 128)), 0.0
+        ).astype(BF16)
         return 0
 
     lax.fori_loop(0, EXPERTS, fill_g, 0)
-    loads["ssm_cache"].wait()
-
-    def fill_b(t, _):
-        f0, f1 = owned(t)
-        b.b_send[t // 8, t % 8, :, 0:CH] = (b.ssm_cache[0] * f0 + b.ssm_cache[1] * f1).astype(BF16)
-        b.b_send[t // 8, t % 8, :, CH : CH + 128] = b.gmat[t // 4]
-        return 0
-
-    lax.fori_loop(0, 32, fill_b, 0)
-
-    for d in x_to:
-        a1[d].wait_recv()
-
-    def mid_a(i, _):
-        total = b.a_send[x, i].astype(F32)
-        for d in (1, 2, 3):
-            total = total + b.a_recv1[d, i].astype(F32)
-        b.a_mid[i] = total.astype(BF16)
-        return 0
-
-    lax.fori_loop(0, 8, mid_a, 0)
-    a2 = {d: send("a2", d, b.a_mid.at[(j + d) % 8], b.a_recv2.at[d], j_to[d], mp) for d in j_to}
-    b1 = {d: send("b1", d, b.b_send.at[(x + d) % 4], b.b_recv1.at[d], x_to[d], mp) for d in x_to}
-
-    loads["xin"].wait()
-    b.xpad[8 : 8 + SUF, :] = b.xin[0].astype(F32)
-    b.d_send[:, :, 256:384] = jnp.zeros((8, 8, 128), F32)
-    for name in ("conv_w", "conv_bias", "x_proj"):
-        loads[name].wait()
+
+    for rel in mp_to:
+        d1[rel].wait_recv()
+    total = b.d_send[z]
+    for rel in mp_to:
+        total = total + b.d_recv[rel]
+    b.d_sum[...] = total
+    b.d_all[z] = total
+    d2 = {
+        dz: send("d2", dz, b.d_sum, b.d_all.at[z], me, mod(z + dz, 8) * 2 + hi)
+        for dz in range(1, 8)
+    }
 
     for d in j_to:
         a2[d].wait_recv()
@@ -291,25 +327,60 @@
         for q in range(4):
             at = 4 * k + q
             b.xpad[5 + k : 6 + k, q * 128 : q * 128 + 128] = b.cs16[at : at + 1, :]
-
-    conv = b.conv_w[0:1, :] * b.xpad[5 : 5 + SUF, :]
-    for k in range(1, 4):
-        conv = conv + b.conv_w[k : k + 1, :] * b.xpad[5 + k : 5 + k + SUF, :]
-    conv = conv + b.conv_bias[...]
-    u16 = silu(conv).astype(BF16)
-    b.u_s[...] = u16.astype(F32)
-    rows_by_rows = (((1,), (1,)), ((), ()))
-    part = lax.dot_general(u16, b.x_proj[0:DTR, :], rows_by_rows, preferred_element_type=F32)
-    part_bc = lax.dot_general(
-        u16, b.x_proj[DTR : DTR + 2 * NS, :], rows_by_rows, preferred_element_type=F32
+    for rel in mp_to:
+        d1[rel].wait_send()
+    pending[:] = [c for c in pending if not any(c is d1[rel] for rel in d1)]
+    project_in(16)
+    tail = b.d_send[0, :, 256:384]
+    b.l_send[...] = jnp.zeros((8, 128), F32)
+    for t in range(3):
+        b.l_send[2 * t : 2 * t + 1, :] = b.d_send[0, t : t + 1, 0:128]
+        b.l_send[2 * t + 1 : 2 * t + 2, :] = b.d_send[0, t : t + 1, 128:256]
+    b.l_send[6:7, :] = (
+        tail[0:1, :] + pltpu.roll(tail, 32, 1)[1:2, :] + pltpu.roll(tail, 64, 1)[2:3, :]
     )
-    b.d_send[:, :, 0:DTR] = part.reshape(8, 8, DTR)
-    b.d_send[:, :, DTR : DTR + 2 * NS] = part_bc.reshape(8, 8, 2 * NS)
-
-    d1 = {
-        rel: send("d1", rel, b.d_send.at[(z + rel // 2) % 8], b.d_recv.at[rel], me, mp_to[rel])
-        for rel in mp_to
+    l1 = {
+        rel: send("l1", rel, b.l_send, b.l_recv.at[rel], me, mp_to[rel]) for rel in mp_to
     }
+
+    loads["ssm_cache"].wait()
+
+    def fill_b(t, _):
+        f0, f1 = owned(t)
+        px, at = lax.div(t, jnp.int32(8)), mod(t, 8)
+        b.b_send[px, at, :, 0:CH] = (b.ssm_cache[0] * f0 + b.ssm_cache[1] * f1).astype(BF16)
+        b.b_send[px, at, :, CH : CH + 128] = b.gmat[lax.div(t, jnp.int32(4))]
+        return 0
+
+    lax.fori_loop(0, 32, fill_b, 0)
+    b1 = {d: send("b1", d, b.b_send.at[x_at[d]], b.b_recv1.at[d], x_to[d], mp) for d in x_to}
+
+    for name in ("dt_proj", "dt_bias", "a_log", "d_skip", "zin"):
+        loads[name].wait()
+    for dz in d2:
+        d2[dz].wait_recv()
+    mask_b = jnp.where(iota((NS, 128), 1) == iota((NS, 128), 0), 1.0, 0.0)
+    mask_c = jnp.where(iota((NS, 128), 1) == iota((NS, 128), 0) + NS, 1.0, 0.0)
+
+    def steps(n):
+        dbc_in = b.d_all[0 : n // 8, :, 0:DTR].reshape(n, DTR).astype(BF16)
+        pre = jnp.dot(dbc_in, b.dt_proj[...], preferred_element_type=F32) + b.dt_bias[...]
+        b.dt_s[0:n, :] = jnp.maximum(pre, 0.0) + jnp.log1p(jnp.exp(-jnp.abs(pre)))
+
+    def spread(i, _):
+        rows = b.d_all[i, :, DTR : DTR + 128]
+        for t in range(8):
+            one = jnp.broadcast_to(rows[t : t + 1, :], (NS, 128))
+            b.b_exp[i * 8 + t] = jnp.broadcast_to(
+                jnp.sum(one * mask_b, axis=1, keepdims=True), (NS, 128)
+            )
+            b.c_exp[i * 8 + t] = jnp.broadcast_to(
+                jnp.sum(one * mask_c, axis=1, keepdims=True), (NS, 128)
+            )
+        return 0
+
+    steps(SUF)
+    lax.fori_loop(1, 8, spread, 0)
 
     for d in x_to:
         b1[d].wait_recv()
@@ -322,31 +393,35 @@
         return 0
 
     lax.fori_loop(0, 8, mid_b, 0)
-    b2 = {d: send("b2", d, b.b_mid.at[(j + d) % 8], b.b_recv2.at[d], j_to[d], mp) for d in j_to}
+    b2 = {d: send("b2", d, b.b_mid.at[j_at[d]], b.b_recv2.at[d], j_to[d], mp) for d in j_to}
 
     for rel in mp_to:
-        d1[rel].wait_recv()
-    total = b.d_send[z]
+        l1[rel].wait_recv()
+    total = b.l_send[...]
     for rel in mp_to:
-        total = total + b.d_recv[rel]
-    b.d_sum[...] = total
-    b.d_all[z] = total
-    d2 = {
-        dz: send("d2", dz, b.d_sum, b.d_all.at[z], me, ((z + dz) % 8) * 2 + hi)
-        for dz in range(1, 8)
-    }
+        total = total + b.l_recv[rel]
+    last = jnp.broadcast_to(total[6:7, :], (8, 128))
+    for t in range(3):
+        b.d_all[0, t : t + 1, 0:128] = total[2 * t : 2 * t + 1, :]
+        b.d_all[0, t : t + 1, 128:256] = total[2 * t + 1 : 2 * t + 2, :]
+        moved = pltpu.roll(last, 128 - 32 * t, 1) if t else last
+        b.d_all[0, t : t + 1, 256:384] = moved[0:1, :]
+    steps(16)
+    spread(0, 0)
 
     for d in (1, 2, 3):
         oy[d].wait_recv()
-        block = b.ow.at[((ylo + 4 - d) % 4) * 2 + core]
+        block = b.ow.at[mod(ylo + 4 - d, 4) * 2 + core]
         osib[d] = send("os", d, block, block, sibling, mp)
 
-    row = iota((256, 1), 0)
-    target = ((row // 4) % 4) * 64 + (row // 16) * 4 + row % 4
-    b.perm_rows[...] = jnp.where(iota((256, 256), 1) == target, 1.0, 0.0).astype(BF16)
     row = iota((128, 1), 0)
+    wide = iota((128, 128), 1)
+    target = ((row // 4) % 4) * 32 + (row // 16) * 4 + row % 4
+    b.perm_rows[...] = jnp.where(wide == target, 1.0, 0.0).astype(BF16)
     target = (row % 16) * 8 + row // 16
-    b.perm_small[...] = jnp.where(iota((128, 128), 1) == target, 1.0, 0.0).astype(BF16)
+    b.perm_small[...] = jnp.where(wide == target, 1.0, 0.0).astype(BF16)
+    target = ((row % 32) // 2) * 8 + (row // 32) * 2 + row % 2
+    b.perm_out[...] = jnp.where(wide == target, 1.0, 0.0).astype(BF16)
     col = iota((1, 32), 1)
     mine = iota((SUF, 1), 0) == mp * 4 + (col // 2) % 4
     col_group = (col // 8) * 2 + col % 2
@@ -375,30 +450,6 @@
                 b.r32[px, at : at + 1, :] = b.r4[t : t + 1, q * 512 : q * 512 + 512]
                 b.g32[px, at : at + 1, :] = b.g8[q : q + 1, :]
 
-    for name in ("dt_proj", "dt_bias", "a_log", "d_skip", "zin"):
-        loads[name].wait()
-    for dz in d2:
-        d2[dz].wait_recv()
-    dbc_in = b.d_all[:, :, 0:DTR].reshape(SUF, DTR).astype(BF16)
-    pre = jnp.dot(dbc_in, b.dt_proj[...], preferred_element_type=F32) + b.dt_bias[...]
-    b.dt_s[...] = jnp.maximum(pre, 0.0) + jnp.log1p(jnp.exp(-jnp.abs(pre)))
-    mask_b = jnp.where(iota((NS, 128), 1) == iota((NS, 128), 0), 1.0, 0.0)
-    mask_c = jnp.where(iota((NS, 128), 1) == iota((NS, 128), 0) + NS, 1.0, 0.0)
-
-    def spread(i, _):
-        rows = b.d_all[i, :, DTR : DTR + 128]
-        for t in range(8):
-            one = jnp.broadcast_to(rows[t : t + 1, :], (NS, 128))
-            b.b_exp[i * 8 + t] = jnp.broadcast_to(
-                jnp.sum(one * mask_b, axis=1, keepdims=True), (NS, 128)
-            )
-            b.c_exp[i * 8 + t] = jnp.broadcast_to(
-                jnp.sum(one * mask_c, axis=1, keepdims=True), (NS, 128)
-            )
-        return 0
-
-    lax.fori_loop(0, 8, spread, 0)
-
     for d in j_to:
         b2[d].wait_recv()
     total = b.b_mid[j].astype(F32)
@@ -422,34 +473,62 @@
             )
         return state
 
-    state = lax.fori_loop(0, 8, scan8, total[:, 0:CH])
-    gated = (b.yv_s[...] + b.d_skip[...] * b.u_s[...]) * silu(b.zin[0].astype(F32))
-    ymix = gated.astype(BF16)
-    b.ymix[...] = ymix
-    b.yfull[x] = ymix
-
-    yx = {d: send("yx", d, b.ymix, b.yfull.at[x], x_to[d], mp) for d in x_to}
-    state_out[...] = state
+    yx = {}
+
+    def mixed(half, state):
+        state = lax.fori_loop(4 * half, 4 * half + 4, scan8, state)
+        at = slice(32 * half, 32 * half + 32)
+        gated = (b.yv_s[at, :] + b.d_skip[...] * b.u_s[at, :]) * silu(b.zin[0, at, :].astype(F32))
+        ymix = gated.astype(BF16)
+        b.ymix[half] = ymix
+        b.yfull[half, x] = ymix
+        for d in x_to:
+            yx[half, d] = send(
+                "yx", (half, d), b.ymix.at[half], b.yfull.at[half, x], x_to[d], mp
+            )
+        return state
+
+    index = mod(mp, 8)
+
+    def project_out(half):
+        for d in x_to:
+            yx[half, d].wait_recv()
+        left = jnp.dot(
+            b.perm_rows[...], b.yfull[half].reshape(128, CH), preferred_element_type=F32
+        ).astype(BF16)
+        for n in range(4):
+            cols = jnp.concatenate([b.ow[2 * n], b.ow[2 * n + 1]], axis=1)
+            part = jnp.dot(left, cols, preferred_element_type=F32).astype(BF16)
+            b.p_send[8 * half : 8 * half + 8, :, n * 256 : n * 256 + 256] = part.reshape(
+                8, 16, 256
+            )
+        apart = half + half_of - 2 * half * half_of
+        for d in range(1, 8):
+            to = 8 * half + mod(index + d, 8)
+            slot = 8 * apart + d
+            send("p", slot, b.p_send.at[to], b.p_recv.at[slot], me, to)
+
+    state = mixed(0, total[:, 0:CH])
+    state = mixed(1, state)
     load_o.wait()
     for d in osib:
         osib[d].wait_recv()
-    for d in x_to:
-        yx[d].wait_recv()
-    left = jnp.dot(
-        b.perm_rows[...], b.yfull[...].reshape(256, CH), preferred_element_type=F32
-    ).astype(BF16)
-    for n in range(4):
-        cols = jnp.concatenate([b.ow[2 * n], b.ow[2 * n + 1]], axis=1)
-        part = jnp.dot(left, cols, preferred_element_type=F32).astype(BF16)
-        b.p_send[:, :, n * 256 : n * 256 + 256] = part.reshape(16, 16, 256)
-    ps = {
-        rel: send("p", rel, b.p_send.at[mp_to[rel]], b.p_recv.at[rel], me, mp_to[rel])
-        for rel in mp_to
-    }
+    project_out(0)
+    project_out(1)
+    across = mod(mp + 8, 16)
+    send("p", 8, b.p_send.at[across], b.p_recv.at[8], me, across)
+    state_out[...] = state
     total = b.p_send[mp].astype(F32)
-    for rel in mp_to:
-        ps[rel].wait_recv()
-        total = total + b.p_recv[rel].astype(F32)
+    for slot in range(1, 16):
+        pltpu.make_async_remote_copy(
+            src_ref=b.p_send.at[0],
+            dst_ref=b.p_recv.at[slot],
+            send_sem=sems["p"][0].at[slot],
+            recv_sem=sems["p"][1].at[slot],
+            device_id=(me, mp),
+            device_id_type=MESH,
+        ).wait_recv()
+        total = total + b.p_recv[slot].astype(F32)
     b.p_sum[...] = total
     for px in range(4):
         for t in range(4):
@@ -458,7 +537,7 @@
                 b.hx_send[px, at : at + 1, :] = b.p_sum[
                     px * 4 + t : px * 4 + t + 1, half * 512 : half * 512 + 512
                 ]
-    hx = {d: send("hx", d, b.hx_send.at[(x + d) % 4], b.hx_recv.at[x], x_to[d], mp) for d in x_to}
+    hx = {d: send("hx", d, b.hx_send.at[x_at[d]], b.hx_recv.at[x], x_to[d], mp) for d in x_to}
     b.hx_recv[x] = b.hx_send[x]
     for d in x_to:
         hx[d].wait_recv()
@@ -483,7 +562,7 @@
 
     ex = {
         d: send(
-            "ex", d, b.e_send.at[pl.ds(2 * ((x + d) % 4), 2)], b.e_mid.at[:, x], x_to[d], mp
+            "ex", d, b.e_send.at[pl.ds(2 * x_at[d], 2)], b.e_mid.at[:, x], x_to[d], mp
         )
         for d in x_to
     }
@@ -498,7 +577,7 @@
     for d in x_to:
         ex[d].wait_recv()
 
-    kind = pair % 2
+    kind = mod(pair, 2)
 
     def send_y(slot, to_y, parity):
         return send(
@@ -506,15 +585,15 @@
             slot * 2 + odd,
             b.e_mid.at[parity],
             b.e_recv.at[slot, odd],
-            req_of(x, to_y % 4, core),
-            z * 2 + to_y // 4,
+            req_of(x, mod(to_y, 4), core),
+            z * 2 + lax.div(to_y, jnp.int32(4)),
         )
 
     send_y(0, yy + 1 - 2 * odd, kind)
-    send_y(1, 2 * ((pair + 1) % 4), 1 - kind)
-    send_y(1, 2 * ((pair + 3) % 4) + 1, 1 - kind)
-    send_y(2, 2 * ((pair + 2) % 4), kind)
-    send_y(2, 2 * ((pair + 2) % 4) + 1, kind)
+    send_y(1, 2 * mod(pair + 1, 4), 1 - kind)
+    send_y(1, 2 * mod(pair + 3, 4) + 1, 1 - kind)
+    send_y(2, 2 * mod(pair + 2, 4), kind)
+    send_y(2, 2 * mod(pair + 2, 4) + 1, kind)
     b.e_recv[0, odd] = b.e_mid[kind]
 
     def got_y(slot, member):
@@ -532,9 +611,9 @@
 
     def ring(way, s, i):
         if way == 0:
-            block, to = (z + 8 - (s - 1)) % 8, (z + 1) % 8
+            block, to = mod(z + 9 - s, 8), mod(z + 1, 8)
         else:
-            block, to = (z + s - 1) % 8, (z + 7) % 8
+            block, to = mod(z + s - 1, 8), mod(z + 7, 8)
         ref = b.xb.at[block, chunk[i], core]
         return send("zr", (way, s, i), ref, ref, me, to * 2 + hi)
 
@@ -549,10 +628,10 @@
         ref = b.xb.at[block, own_side, core]
         return send("pr", row, ref, ref, partner, mp)
 
-    block_of = {0: z, 7: (z + 4) % 8}
+    block_of = {0: z, 7: mod(z + 4, 8)}
     for s in (1, 2, 3):
-        block_of[2 * s - 1] = (z + 8 - s) % 8
-        block_of[2 * s] = (z + s) % 8
+        block_of[2 * s - 1] = mod(z + 8 - s, 8)
+        block_of[2 * s] = mod(z + s, 8)
 
     zr, zs, pr = {}, {}, {}
     for i in range(3):
@@ -629,7 +708,7 @@
                 for c in range(2):
                     for member in range(2):
                         at = g * 32 + c * 16 + member * 8
-                        act_out[block, (2 * pair + 2 * g + member) % 8, c] = act[at : at + 8, :]
+                        b.act_s[block, mod(2 * pair + 2 * g + member, 8), c] = act[at : at + 8, :]
 
     loads["w_gate"].wait()
     loads["w_up"].wait()
@@ -637,8 +716,8 @@
         for i in range(3):
             handle(s, i)
         if s == 3:
-            ref = b.xb.at[(z + 5 + core * 6) % 8, 2, core]
-            z4 = send("z4", 0, ref, ref, me, ((z + 1 + core * 6) % 8) * 2 + hi)
+            ref = b.xb.at[mod(z + 5 + core * 6, 8), 2, core]
+            z4 = send("z4", 0, ref, ref, me, mod(z + 1 + core * 6, 8) * 2 + hi)
         from_pair([0] if s == 1 else [2 * s - 3, 2 * s - 2])
         if s == 2:
             expert([0])
@@ -653,6 +732,16 @@
     expert([5, 6])
     from_pair([7])
     expert([7])
+
+    for line in range(4):
+        for c in range(2):
+            rows = jnp.concatenate(
+                [b.act_s[pz, ph * 4 + line, c] for pz in range(8) for ph in range(2)], axis=0
+            ).astype(BF16)
+            rows = jnp.dot(b.perm_out[...], rows, preferred_element_type=F32).astype(BF16)
+            for px in range(4):
+                at = ((px * 4 + line) * 2 + c) * 32
+                act_out[at : at + 32, :] = rows[px * 32 : px * 32 + 32, :]
 
     for copy in pending:
         copy.wait_send()
@@ -711,7 +800,7 @@
         out_shape=(
             jax.ShapeDtypeStruct((4, D), BF16),
             jax.ShapeDtypeStruct((NS, CH), F32),
-            jax.ShapeDtypeStruct((8, 8, 2, 8, HID), F32),
+            jax.ShapeDtypeStruct((1024, HID), BF16),
         ),
         in_specs=[pl.BlockSpec(memory_space=pltpu.HBM)] * len(OPERANDS),
         out_specs=(vmem, vmem, vmem),
@@ -721,8 +810,7 @@
         ),
         name="mixer_and_experts",
     )(*[operands[name] for name in OPERANDS])
-    act = act.reshape(8, 2, 4, 2, 4, 2, HID).transpose(4, 2, 3, 0, 1, 5, 6)
-    return (stream, state[None], act.astype(BF16).reshape(1, 1024, HID))
+    return (stream, state[None], act[None])
 
 
 def solution(mesh):

time: 127 us -> 127 us (level)
  local copies, waits for them, and re-layouts: 2.97 us -> 4.63 us
  other arithmetic: 1.3 us -> 0 us
    unnamed x6 -> x3, local copies, waits for them, and re-layouts: 1.24 us -> 4.63 us
    convert_element_type x1 -> x0, other arithmetic: 1.3 us -> none  [local(): return (stream, state[None], act.astype(BF16).reshape(1, 1024, HID))]
where the time goes in v3:
time: 127 us; the launch traced here: 126 us
  Pallas kernels  121 us (95%)
  local copies, waits for them, and re-layouts  4.63 us (4%)
    pallas_call x1, Pallas kernels, local(): pl.pallas_call(kernel, out_shape=(jax.ShapeDtypeStruct((4, D), BF16), jax...  121 us
    unnamed x3, local copies, waits for them, and re-layouts  4.63 us

profile of v3, /device:TPU:1, one launch (start us, length us, event | category | flops | bytes accessed | tf_op | source)
XLA Modules:
  0.0 126.0 jit_solution(10938224254949974343)
XLA Ops:
  0.6 120.7 %mixer_and_experts.1 = (bf16[4,4096]{1,0:T(4,128)(2,1)}, f32[16,512]{1,0:T(8,128)}, bf16[1024,256]{1,0:T(8,128)(2,1)}) custom-call(s32[32]{0:T(128)} %refs_0_.1, f32[3,2,512]{2,1,0:T(2,128)} %bitcast.14, s32[2,64]{1,0:T(2,128)} %bitcast.18, bf16[2,64]{1,0:T(2,128)(2,1)} %bitcast.19, f32[2,16,512]{2,1,0:T(8,128)} %refs_4_.1, bf16[1,64,512]{2,1,0:T(8,128)(2,1)} %refs_5_.1, ...), custom_call_target="tpu_custom_call" | custom-call | tf_op jit(solution)/shard_map/mixer_and_experts/pallas_call | solution.py:798
  121.3 1.4 %copy.25 = bf16[4,4096]{1,0:T(4,128)(2,1)} copy(bf16[4,4096]{1,0:T(4,128)(2,1)} %get-tuple-element.12) | data formatting | bytes 65536
  122.7 1.4 %copy.26 = f32[1,16,512]{2,1,0:T(8,128)} copy(f32[1,16,512]{2,1,0:T(8,128)} %bitcast.12) | data formatting | bytes 65536
  124.1 1.9 %copy.27 = bf16[1,1024,256]{2,1,0:T(8,128)(2,1)} copy(bf16[1,1024,256]{2,1,0:T(8,128)(2,1)} %bitcast.10) | data formatting | bytes 1048576

commit v4 on v3

--- a/solution.py
+++ b/solution.py
@@ -45,17 +45,18 @@
     "cc16": VMEM((2, 16, 128), F32),
     "cs16": VMEM((16, 128), F32),
     "xpad": VMEM((72, CH), F32),
-    "a_send": VMEM((4, 8, 16, 128), BF16),
-    "a_recv1": VMEM((4, 8, 16, 128), BF16),
+    "c_send": VMEM((2, 16, CH + 128), BF16),
+    "c_recv": VMEM((4, 2, 16, CH + 128), BF16),
+    "g_recv": VMEM((4, 2, 16, 128), BF16),
     "a_mid": VMEM((8, 16, 128), BF16),
     "a_recv2": VMEM((8, 16, 128), BF16),
-    "b_send": VMEM((4, 8, 16, CH + 128), BF16),
-    "b_recv1": VMEM((4, 8, 16, CH + 128), BF16),
     "b_mid": VMEM((8, 16, CH + 128), BF16),
     "b_recv2": VMEM((8, 16, CH + 128), BF16),
     "gmat": VMEM((8, 16, 128), BF16),
     "d_send": VMEM((8, 8, 384), F32),
-    "d_recv": VMEM((16, 8, 384), F32),
+    "d_recv": VMEM((8, 8, 384), F32),
+    "d_part": VMEM((8, 384), F32),
+    "d_other": VMEM((8, 384), F32),
     "d_sum": VMEM((8, 384), F32),
     "d_all": VMEM((8, 8, 384), F32),
     "l_send": VMEM((8, 128), F32),
@@ -72,7 +73,10 @@
     "perm_out": VMEM((128, 128), BF16),
     "perm_small": VMEM((128, 128), BF16),
     "p_send": VMEM((16, 16, 1024), BF16),
-    "p_recv": VMEM((16, 16, 1024), BF16),
+    "p_recv": VMEM((8, 2, 16, 1024), BF16),
+    "p_relay": VMEM((2, 16, 1024), BF16),
+    "p_part": VMEM((16, 1024), BF16),
+    "p_other": VMEM((16, 1024), BF16),
     "p_sum": VMEM((16, 1024), F32),
     "hx_send": VMEM((4, 8, 512), F32),
     "hx_recv": VMEM((4, 8, 512), F32),
@@ -92,17 +96,19 @@
     "act_s": VMEM((8, 8, 2, 8, HID), F32),
 }
 COPIES = {
-    "a1": (4,),
+    "c1": (4,),
+    "g1": (4,),
     "a2": (8,),
-    "b1": (4,),
     "b2": (8,),
-    "d1": (16,),
+    "d1": (8,),
+    "dy": (1,),
     "d2": (8,),
     "l1": (16,),
     "oy": (4,),
     "os": (4,),
     "yx": (2, 4),
-    "p": (16,),
+    "p": (8,),
+    "py": (1,),
     "hx": (4,),
     "ex": (4,),
     "ey": (6,),
@@ -148,7 +154,8 @@
     yy = hi * 4 + ylo
     odd = mod(ylo, 2)
     pair = lax.div(yy, jnp.int32(2))
-    half_of = lax.div(z, jnp.int32(4))
+    z_at = {dz: mod(z + dz, 8) for dz in range(1, 8)}
+    over_y = z * 2 + 1 - hi
 
     def req_of(px, pylo, pcore):
         return px * 8 + pylo * 2 + pcore
@@ -204,67 +211,11 @@
                 at = 4 * k + q
                 b.cc16[s, at : at + 1, :] = b.conv_cache[k, s : s + 1, q * 128 : q * 128 + 128]
 
-    def owned(t):
-        p = b.prefix_of[t]
-        f0 = jnp.where(p == 2 * me, 1.0, 0.0).astype(F32)
-        f1 = jnp.where(p == 2 * me + 1, 1.0, 0.0).astype(F32)
-        return f0, f1
-
-    def fill_a(t, _):
-        f0, f1 = owned(t)
-        b.a_send[t // 8, t % 8] = (b.cc16[0] * f0 + b.cc16[1] * f1).astype(BF16)
-        return 0
-
-    lax.fori_loop(0, 32, fill_a, 0)
-    pl.semaphore_wait(barrier, len(greet))
-
-    a1 = {d: send("a1", d, b.a_send.at[x_at[d]], b.a_recv1.at[d], x_to[d], mp) for d in x_to}
-
-    loads["xin"].wait()
-    b.xpad[0:8, :] = jnp.zeros((8, CH), F32)
-    b.xpad[8 : 8 + SUF, :] = b.xin[0].astype(F32)
-    b.d_send[:, :, 256:384] = jnp.zeros((8, 8, 128), F32)
-    for name in ("conv_w", "conv_bias", "x_proj"):
-        loads[name].wait()
-    rows_by_rows = (((1,), (1,)), ((), ()))
-
-    def project_in(n):
-        conv = b.conv_w[0:1, :] * b.xpad[5 : 5 + n, :]
-        for k in range(1, 4):
-            conv = conv + b.conv_w[k : k + 1, :] * b.xpad[5 + k : 5 + k + n, :]
-        u16 = silu(conv + b.conv_bias[...]).astype(BF16)
-        b.u_s[0:n, :] = u16.astype(F32)
-        part = lax.dot_general(u16, b.x_proj[0:DTR, :], rows_by_rows, preferred_element_type=F32)
-        part_bc = lax.dot_general(
-            u16, b.x_proj[DTR : DTR + 2 * NS, :], rows_by_rows, preferred_element_type=F32
-        )
-        b.d_send[0 : n // 8, :, 0:DTR] = part.reshape(n // 8, 8, DTR)
-        b.d_send[0 : n // 8, :, DTR : DTR + 2 * NS] = part_bc.reshape(n // 8, 8, 2 * NS)
-
-    project_in(SUF)
-    d1 = {
-        rel: send("d1", rel, b.d_send.at[mod(z + rel // 2, 8)], b.d_recv.at[rel], me, mp_to[rel])
-        for rel in mp_to
-    }
-
-    for d in x_to:
-        a1[d].wait_recv()
-
-    def mid_a(i, _):
-        total = b.a_send[x, i].astype(F32)
-        for d in (1, 2, 3):
-            total = total + b.a_recv1[d, i].astype(F32)
-        b.a_mid[i] = total.astype(BF16)
-        return 0
-
-    lax.fori_loop(0, 8, mid_a, 0)
-    a2 = {d: send("a2", d, b.a_mid.at[j_at[d]], b.a_recv2.at[d], j_to[d], mp) for d in j_to}
-
-    oy = {}
-    for d in (1, 2, 3):
-        to = req_of(x, mod(ylo + d, 4), core)
-        oy[d] = send("oy", d, hbm["out_w"], b.ow.at[j], to, mp)
-    osib = {0: send("os", 0, hbm["out_w"], b.ow.at[j], sibling, mp)}
+    loads["ssm_cache"].wait()
+    for s in range(2):
+        b.c_send[s, :, 0:CH] = b.ssm_cache[s].astype(BF16)
+        b.c_send[s, :, CH : CH + 128] = b.cc16[s].astype(BF16)
+    b.c_recv[0] = b.c_send[...]
 
     loads["ids"].wait()
     loads["gate_w"].wait()
@@ -305,16 +256,96 @@
 
     lax.fori_loop(0, EXPERTS, fill_g, 0)
 
-    for rel in mp_to:
-        d1[rel].wait_recv()
+    b.g_recv[0, 0] = b.gmat[2 * x]
+    b.g_recv[0, 1] = b.gmat[2 * x + 1]
+
+    loads["xin"].wait()
+    b.xpad[0:8, :] = jnp.zeros((8, CH), F32)
+    b.xpad[8 : 8 + SUF, :] = b.xin[0].astype(F32)
+    b.d_send[:, :, 256:384] = jnp.zeros((8, 8, 128), F32)
+    for name in ("conv_w", "conv_bias", "x_proj"):
+        loads[name].wait()
+    rows_by_rows = (((1,), (1,)), ((), ()))
+
+    def project_in(n):
+        conv = b.conv_w[0:1, :] * b.xpad[5 : 5 + n, :]
+        for k in range(1, 4):
+            conv = conv + b.conv_w[k : k + 1, :] * b.xpad[5 + k : 5 + k + n, :]
+        u16 = silu(conv + b.conv_bias[...]).astype(BF16)
+        b.u_s[0:n, :] = u16.astype(F32)
+        part = lax.dot_general(u16, b.x_proj[0:DTR, :], rows_by_rows, preferred_element_type=F32)
+        part_bc = lax.dot_general(
+            u16, b.x_proj[DTR : DTR + 2 * NS, :], rows_by_rows, preferred_element_type=F32
+        )
+        b.d_send[0 : n // 8, :, 0:DTR] = part.reshape(n // 8, 8, DTR)
+        b.d_send[0 : n // 8, :, DTR : DTR + 2 * NS] = part_bc.reshape(n // 8, 8, 2 * NS)
+
+    project_in(SUF)
+    pl.semaphore_wait(barrier, len(greet))
+    c1 = {d: send("c1", d, b.c_send, b.c_recv.at[d], x_to[d], mp) for d in x_to}
+    d1 = {
+        dz: send("d1", dz, b.d_send.at[z_at[dz]], b.d_recv.at[dz], me, z_at[dz] * 2 + hi)
+        for dz in z_at
+    }
+    g1 = {
+        d: send("g1", d, b.gmat.at[pl.ds(2 * x_at[d], 2)], b.g_recv.at[d], x_to[d], mp)
+        for d in x_to
+    }
+
+    across_y = mod(ylo + 2, 4)
+    beside_y = ylo + 1 - 2 * odd
+    oy = {
+        1: send("oy", 1, hbm["out_w"], b.ow.at[j], req_of(x, across_y, core), mp),
+        2: send("oy", 2, hbm["out_w"], b.ow.at[j], partner, mp),
+    }
+    osib = {0: send("os", 0, hbm["out_w"], b.ow.at[j], sibling, mp)}
+
+    for d in x_to:
+        c1[d].wait_recv()
+
+    def chosen_prefix(i, lanes):
+        p = b.prefix_of[x * 8 + i]
+        total = jnp.zeros((16, lanes.stop - lanes.start), F32)
+        for d in range(4):
+            owner = mod(x + 4 - d, 4) * 8 + j
+            for s in range(2):
+                here = jnp.where(p == 2 * owner + s, 1.0, 0.0).astype(F32)
+                total = total + b.c_recv[d, s, :, lanes].astype(F32) * here
+        return total.astype(BF16)
+
+    def mid_a(i, _):
+        b.a_mid[i] = chosen_prefix(i, slice(CH, CH + 128))
+        return 0
+
+    lax.fori_loop(0, 8, mid_a, 0)
+    a2 = {d: send("a2", d, b.a_mid.at[j_at[d]], b.a_recv2.at[d], j_to[d], mp) for d in j_to}
+    for d in x_to:
+        g1[d].wait_recv()
+
+    def mid_b(i, _):
+        b.b_mid[i, :, 0:CH] = chosen_prefix(i, slice(0, CH))
+        total = b.g_recv[0, lax.div(i, jnp.int32(4))].astype(F32)
+        for d in (1, 2, 3):
+            total = total + b.g_recv[d, lax.div(i, jnp.int32(4))].astype(F32)
+        b.b_mid[i, :, CH : CH + 128] = total.astype(BF16)
+        return 0
+
+    lax.fori_loop(0, 8, mid_b, 0)
+    b2 = {d: send("b2", d, b.b_mid.at[j_at[d]], b.b_recv2.at[d], j_to[d], mp) for d in j_to}
+
+    for dz in d1:
+        d1[dz].wait_recv()
     total = b.d_send[z]
-    for rel in mp_to:
-        total = total + b.d_recv[rel]
+    for dz in d1:
+        total = total + b.d_recv[dz]
+    b.d_part[...] = total
+    dy = send("dy", 0, b.d_part, b.d_other, me, over_y)
+    dy.wait_recv()
+    total = total + b.d_other[...]
     b.d_sum[...] = total
     b.d_all[z] = total
     d2 = {
-        dz: send("d2", dz, b.d_sum, b.d_all.at[z], me, mod(z + dz, 8) * 2 + hi)
-        for dz in range(1, 8)
+        dz: send("d2", dz, b.d_sum, b.d_all.at[z], me, z_at[dz] * 2 + hi) for dz in z_at
     }
 
     for d in j_to:
@@ -327,9 +358,9 @@
         for q in range(4):
             at = 4 * k + q
             b.xpad[5 + k : 6 + k, q * 128 : q * 128 + 128] = b.cs16[at : at + 1, :]
-    for rel in mp_to:
-        d1[rel].wait_send()
-    pending[:] = [c for c in pending if not any(c is d1[rel] for rel in d1)]
+    for dz in d1:
+        d1[dz].wait_send()
+    pending[:] = [c for c in pending if not any(c is d1[dz] for dz in d1)]
     project_in(16)
     tail = b.d_send[0, :, 256:384]
     b.l_send[...] = jnp.zeros((8, 128), F32)
@@ -343,17 +374,10 @@
         rel: send("l1", rel, b.l_send, b.l_recv.at[rel], me, mp_to[rel]) for rel in mp_to
     }
 
-    loads["ssm_cache"].wait()
-
-    def fill_b(t, _):
-        f0, f1 = owned(t)
-        px, at = lax.div(t, jnp.int32(8)), mod(t, 8)
-        b.b_send[px, at, :, 0:CH] = (b.ssm_cache[0] * f0 + b.ssm_cache[1] * f1).astype(BF16)
-        b.b_send[px, at, :, CH : CH + 128] = b.gmat[lax.div(t, jnp.int32(4))]
-        return 0
-
-    lax.fori_loop(0, 32, fill_b, 0)
-    b1 = {d: send("b1", d, b.b_send.at[x_at[d]], b.b_recv1.at[d], x_to[d], mp) for d in x_to}
+    oy[1].wait_recv()
+    block = b.ow.at[across_y * 2 + core]
+    oy[3] = send("oy", 3, block, block, partner, mp)
+    osib[1] = send("os", 1, block, block, sibling, mp)
 
     for name in ("dt_proj", "dt_bias", "a_log", "d_skip", "zin"):
         loads[name].wait()
@@ -381,19 +405,6 @@
 
     steps(SUF)
     lax.fori_loop(1, 8, spread, 0)
-
-    for d in x_to:
-        b1[d].wait_recv()
-
-    def mid_b(i, _):
-        total = b.b_send[x, i].astype(F32)
-        for d in (1, 2, 3):
-            total = total + b.b_recv1[d, i].astype(F32)
-        b.b_mid[i] = total.astype(BF16)
-        return 0
-
-    lax.fori_loop(0, 8, mid_b, 0)
-    b2 = {d: send("b2", d, b.b_mid.at[j_at[d]], b.b_recv2.at[d], j_to[d], mp) for d in j_to}
 
     for rel in mp_to:
         l1[rel].wait_recv()
@@ -409,10 +420,10 @@
     steps(16)
     spread(0, 0)
 
-    for d in (1, 2, 3):
-        oy[d].wait_recv()
-        block = b.ow.at[mod(ylo + 4 - d, 4) * 2 + core]
-        osib[d] = send("os", d, block, block, sibling, mp)
+    for n, line in ((2, beside_y), (3, mod(beside_y + 2, 4))):
+        oy[n].wait_recv()
+        block = b.ow.at[line * 2 + core]
+        osib[n] = send("os", n, block, block, sibling, mp)
 
     row = iota((128, 1), 0)
     wide = iota((128, 128), 1)
@@ -488,8 +499,6 @@
             )
         return state
 
-    index = mod(mp, 8)
-
     def project_out(half):
         for d in x_to:
             yx[half, d].wait_recv()
@@ -502,11 +511,6 @@
             b.p_send[8 * half : 8 * half + 8, :, n * 256 : n * 256 + 256] = part.reshape(
                 8, 16, 256
             )
-        apart = half + half_of - 2 * half * half_of
-        for d in range(1, 8):
-            to = 8 * half + mod(index + d, 8)
-            slot = 8 * apart + d
-            send("p", slot, b.p_send.at[to], b.p_recv.at[slot], me, to)
 
     state = mixed(0, total[:, 0:CH])
     state = mixed(1, state)
@@ -515,20 +519,32 @@
         osib[d].wait_recv()
     project_out(0)
     project_out(1)
-    across = mod(mp + 8, 16)
-    send("p", 8, b.p_send.at[across], b.p_recv.at[8], me, across)
+
+    def send_p(name, at, to_z, dst, dz):
+        src = b.p_send.at[pl.ds(2 * to_z, 2)]
+        return send(name, at, src, dst, me, z_at[dz] * 2 + hi)
+
+    relay = send_p("p", 4, z_at[4], b.p_relay, 7)
+    ps = {dz: send_p("p", dz, z_at[dz], b.p_recv.at[dz], dz) for dz in (3, 6, 2, 7, 1)}
+    relay.wait_recv()
+    at = pl.ds(2 * z_at[5], 2)
+    b.p_send[at] = (b.p_send[at].astype(F32) + b.p_relay[...].astype(F32)).astype(BF16)
+    ps[5] = send_p("p", 5, z_at[5], b.p_recv.at[5], 5)
     state_out[...] = state
-    total = b.p_send[mp].astype(F32)
-    for slot in range(1, 16):
-        pltpu.make_async_remote_copy(
-            src_ref=b.p_send.at[0],
-            dst_ref=b.p_recv.at[slot],
-            send_sem=sems["p"][0].at[slot],
-            recv_sem=sems["p"][1].at[slot],
-            device_id=(me, mp),
-            device_id_type=MESH,
-        ).wait_recv()
-        total = total + b.p_recv[slot].astype(F32)
+    for dz in (1, 7, 2, 6, 3, 5):
+        ps[dz].wait_recv()
+
+    def part_sum(row):
+        total = b.p_send[2 * z + row].astype(F32)
+        for dz in ps:
+            total = total + b.p_recv[dz, row].astype(F32)
+        return total
+
+    b.p_part[...] = part_sum(1 - hi).astype(BF16)
+    py = send("py", 0, b.p_part, b.p_other, me, over_y)
+    total = part_sum(hi)
+    py.wait_recv()
+    total = total + b.p_other[...].astype(F32)
     b.p_sum[...] = total
     for px in range(4):
         for t in range(4):
@@ -745,6 +761,19 @@
 
     for copy in pending:
         copy.wait_send()
+
+
+def finish(*refs):
+    ins, outs, held, sems = refs[0:3], refs[3:6], refs[6:9], refs[9]
+    taken = [pltpu.make_async_copy(ins[n], held[n], sems.at[n]) for n in range(3)]
+    given = [pltpu.make_async_copy(held[n], outs[n], sems.at[3 + n]) for n in range(3)]
+    for copy in taken:
+        copy.start()
+    for n in range(3):
+        taken[n].wait()
+        given[n].start()
+    for copy in given:
+        copy.wait()
 
 
 def local(
@@ -795,13 +824,14 @@
     for shape in COPIES.values():
         sems += [dma(shape), dma(shape)]
     sems.append(dma((len(LOADED) + 1,)))
-    stream, state, act = pl.pallas_call(
+    results = (
+        jax.ShapeDtypeStruct((4, D), BF16),
+        jax.ShapeDtypeStruct((NS, CH), F32),
+        jax.ShapeDtypeStruct((1024, HID), BF16),
+    )
+    made = pl.pallas_call(
         kernel,
-        out_shape=(
-            jax.ShapeDtypeStruct((4, D), BF16),
-            jax.ShapeDtypeStruct((NS, CH), F32),
-            jax.ShapeDtypeStruct((1024, HID), BF16),
-        ),
+        out_shape=results,
         in_specs=[pl.BlockSpec(memory_space=pltpu.HBM)] * len(OPERANDS),
         out_specs=(vmem, vmem, vmem),
         scratch_shapes=list(LOADED.values()) + list(SCRATCH.values()) + sems,
@@ -810,6 +840,16 @@
         ),
         name="mixer_and_experts",
     )(*[operands[name] for name in OPERANDS])
+    in_hbm = [pl.BlockSpec(memory_space=pltpu.HBM)] * 3
+    stream, state, act = pl.pallas_call(
+        finish,
+        out_shape=results,
+        in_specs=in_hbm,
+        out_specs=in_hbm,
+        scratch_shapes=[VMEM(r.shape, r.dtype) for r in results] + [dma((6,))],
+        compiler_params=pltpu.CompilerParams(vmem_limit_bytes=60 * 1024 * 1024),
+        name="results",
+    )(*made)
     return (stream, state[None], act[None])
 
 

time: 127 us -> 113 us (0.89)
  Pallas kernels: 121 us -> 112 us
  local copies, waits for them, and re-layouts: 4.63 us -> 0 us
    pallas_call x1 -> x2, Pallas kernels: 121 us -> 112 us  [the longest x1 110 us: local(): pl.pallas_call(kernel, out_shape=results, in_specs=[pl.BlockSpec(memory_s...]
    unnamed x3 -> x0, local copies, waits for them, and re-layouts: 4.63 us -> none
where the time goes in v4:
time: 113 us; the launch traced here: 112 us
  Pallas kernels  112 us (99%)
    pallas_call x1, Pallas kernels, local(): pl.pallas_call(kernel, out_shape=results, in_specs=[pl.BlockSpec(memory_s...  110 us

profile of v4, /device:TPU:1, one launch (start us, length us, event | category | flops | bytes accessed | tf_op | source)
XLA Modules:
  0.0 112.4 jit_solution(5827040426054715196)
XLA Ops:
  0.6 109.9 %mixer_and_experts.1 = (bf16[4,4096]{1,0:T(4,128)(2,1)}, f32[16,512]{1,0:T(8,128)}, bf16[1024,256]{1,0:T(8,128)(2,1)}) custom-call(s32[32]{0:T(128)} %refs_0_.1, f32[3,2,512]{2,1,0:T(2,128)} %bitcast.12, s32[2,64]{1,0:T(2,128)} %bitcast.16, bf16[2,64]{1,0:T(2,128)(2,1)} %bitcast.17, f32[2,16,512]{2,1,0:T(8,128)} %refs_4_.1, bf16[1,64,512]{2,1,0:T(8,128)(2,1)} %refs_5_.1, ...), custom_call_target="tpu_custom_call" | custom-call | tf_op jit(solution)/shard_map/mixer_and_experts/pallas_call | solution.py:832
  110.5 1.9 %results.1 = (bf16[4,4096]{1,0:T(4,128)(2,1)}, f32[16,512]{1,0:T(8,128)}, bf16[1024,256]{1,0:T(8,128)(2,1)}) custom-call(bf16[4,4096]{1,0:T(4,128)(2,1)} %get-tuple-element.9.refs_0_, f32[16,512]{1,0:T(8,128)} %get-tuple-element.10.refs_1_, bf16[1024,256]{1,0:T(8,128)(2,1)} %get-tuple-element.11.refs_2_), custom_call_target="tpu_custom_call" | custom-call | tf_op jit(solution)/shard_map/results/pallas_call | solution.py:844

commit v5 on v4

--- a/solution.py
+++ b/solution.py
@@ -217,6 +217,42 @@
         b.c_send[s, :, CH : CH + 128] = b.cc16[s].astype(BF16)
     b.c_recv[0] = b.c_send[...]
 
+    loads["xin"].wait()
+    b.xpad[0:8, :] = jnp.zeros((8, CH), F32)
+    b.xpad[8 : 8 + SUF, :] = b.xin[0].astype(F32)
+    b.d_send[:, :, 256:384] = jnp.zeros((8, 8, 128), F32)
+    for name in ("conv_w", "conv_bias", "x_proj"):
+        loads[name].wait()
+    rows_by_rows = (((1,), (1,)), ((), ()))
+
+    def project_in(n):
+        conv = b.conv_w[0:1, :] * b.xpad[5 : 5 + n, :]
+        for k in range(1, 4):
+            conv = conv + b.conv_w[k : k + 1, :] * b.xpad[5 + k : 5 + k + n, :]
+        u16 = silu(conv + b.conv_bias[...]).astype(BF16)
+        b.u_s[0:n, :] = u16.astype(F32)
+        part = lax.dot_general(u16, b.x_proj[0:DTR, :], rows_by_rows, preferred_element_type=F32)
+        part_bc = lax.dot_general(
+            u16, b.x_proj[DTR : DTR + 2 * NS, :], rows_by_rows, preferred_element_type=F32
+        )
+        b.d_send[0 : n // 8, :, 0:DTR] = part.reshape(n // 8, 8, DTR)
+        b.d_send[0 : n // 8, :, DTR : DTR + 2 * NS] = part_bc.reshape(n // 8, 8, 2 * NS)
+
+    project_in(SUF)
+    pl.semaphore_wait(barrier, len(greet))
+    c1 = {d: send("c1", d, b.c_send, b.c_recv.at[d], x_to[d], mp) for d in x_to}
+    d1 = {
+        dz: send("d1", dz, b.d_send.at[z_at[dz]], b.d_recv.at[dz], me, z_at[dz] * 2 + hi)
+        for dz in z_at
+    }
+    across_y = mod(ylo + 2, 4)
+    beside_y = ylo + 1 - 2 * odd
+    oy = {
+        1: send("oy", 1, hbm["out_w"], b.ow.at[j], req_of(x, across_y, core), mp),
+        2: send("oy", 2, hbm["out_w"], b.ow.at[j], partner, mp),
+    }
+    osib = {0: send("os", 0, hbm["out_w"], b.ow.at[j], sibling, mp)}
+
     loads["ids"].wait()
     loads["gate_w"].wait()
     eye = iota((SUF, SUF), 0) == iota((SUF, SUF), 1)
@@ -259,46 +295,10 @@
     b.g_recv[0, 0] = b.gmat[2 * x]
     b.g_recv[0, 1] = b.gmat[2 * x + 1]
 
-    loads["xin"].wait()
-    b.xpad[0:8, :] = jnp.zeros((8, CH), F32)
-    b.xpad[8 : 8 + SUF, :] = b.xin[0].astype(F32)
-    b.d_send[:, :, 256:384] = jnp.zeros((8, 8, 128), F32)
-    for name in ("conv_w", "conv_bias", "x_proj"):
-        loads[name].wait()
-    rows_by_rows = (((1,), (1,)), ((), ()))
-
-    def project_in(n):
-        conv = b.conv_w[0:1, :] * b.xpad[5 : 5 + n, :]
-        for k in range(1, 4):
-            conv = conv + b.conv_w[k : k + 1, :] * b.xpad[5 + k : 5 + k + n, :]
-        u16 = silu(conv + b.conv_bias[...]).astype(BF16)
-        b.u_s[0:n, :] = u16.astype(F32)
-        part = lax.dot_general(u16, b.x_proj[0:DTR, :], rows_by_rows, preferred_element_type=F32)
-        part_bc = lax.dot_general(
-            u16, b.x_proj[DTR : DTR + 2 * NS, :], rows_by_rows, preferred_element_type=F32
-        )
-        b.d_send[0 : n // 8, :, 0:DTR] = part.reshape(n // 8, 8, DTR)
-        b.d_send[0 : n // 8, :, DTR : DTR + 2 * NS] = part_bc.reshape(n // 8, 8, 2 * NS)
-
-    project_in(SUF)
-    pl.semaphore_wait(barrier, len(greet))
-    c1 = {d: send("c1", d, b.c_send, b.c_recv.at[d], x_to[d], mp) for d in x_to}
-    d1 = {
-        dz: send("d1", dz, b.d_send.at[z_at[dz]], b.d_recv.at[dz], me, z_at[dz] * 2 + hi)
-        for dz in z_at
-    }
     g1 = {
         d: send("g1", d, b.gmat.at[pl.ds(2 * x_at[d], 2)], b.g_recv.at[d], x_to[d], mp)
         for d in x_to
     }
-
-    across_y = mod(ylo + 2, 4)
-    beside_y = ylo + 1 - 2 * odd
-    oy = {
-        1: send("oy", 1, hbm["out_w"], b.ow.at[j], req_of(x, across_y, core), mp),
-        2: send("oy", 2, hbm["out_w"], b.ow.at[j], partner, mp),
-    }
-    osib = {0: send("os", 0, hbm["out_w"], b.ow.at[j], sibling, mp)}
 
     for d in x_to:
         c1[d].wait_recv()
@@ -608,8 +608,7 @@
     send_y(0, yy + 1 - 2 * odd, kind)
     send_y(1, 2 * mod(pair + 1, 4), 1 - kind)
     send_y(1, 2 * mod(pair + 3, 4) + 1, 1 - kind)
-    send_y(2, 2 * mod(pair + 2, 4), kind)
-    send_y(2, 2 * mod(pair + 2, 4) + 1, kind)
+    send_y(2, 2 * mod(pair + 2, 4) + 1 - odd, kind)
     b.e_recv[0, odd] = b.e_mid[kind]
 
     def got_y(slot, member):
@@ -653,9 +652,14 @@
     for i in range(3):
         if i == 0:
             got_y(0, 1 - odd)
+        elif i == 1:
+            got_y(1, 0)
+            got_y(1, 1)
         else:
-            got_y(i, 0)
-            got_y(i, 1)
+            got_y(2, 1 - odd)
+            block = b.e_recv.at[2, 1 - odd]
+            send("ey", 5 - odd, block, block, partner, mp)
+            got_y(2, odd)
         raw = b.e_recv[i].reshape(128, 512)
         rows = jnp.dot(b.perm_small[...], raw, preferred_element_type=F32).astype(BF16)
         for q in range(8):

time: 113 us -> 114 us (level)
    pallas_call x1, Pallas kernels: 110 us -> 112 us  [local(): pl.pallas_call(kernel, out_shape=results, in_specs=[pl.BlockSpec(memory_s...]
where the time goes in v5:
time: 114 us
  Pallas kernels  113 us (99%)
    pallas_call x1, Pallas kernels, local(): pl.pallas_call(kernel, out_shape=results, in_specs=[pl.BlockSpec(memory_s...  112 us

profile of v5, /device:TPU:1, one launch (start us, length us, event | category | flops | bytes accessed | tf_op | source)
XLA Modules:
  0.0 114.1 jit_solution(16503773709618509625)
XLA Ops:
  0.6 111.6 %mixer_and_experts.1 = (bf16[4,4096]{1,0:T(4,128)(2,1)}, f32[16,512]{1,0:T(8,128)}, bf16[1024,256]{1,0:T(8,128)(2,1)}) custom-call(s32[32]{0:T(128)} %refs_0_.1, f32[3,2,512]{2,1,0:T(2,128)} %bitcast.12, s32[2,64]{1,0:T(2,128)} %bitcast.16, bf16[2,64]{1,0:T(2,128)(2,1)} %bitcast.17, f32[2,16,512]{2,1,0:T(8,128)} %refs_4_.1, bf16[1,64,512]{2,1,0:T(8,128)(2,1)} %refs_5_.1, ...), custom_call_target="tpu_custom_call" | custom-call | tf_op jit(solution)/shard_map/mixer_and_experts/pallas_call | solution.py:836
  112.2 1.9 %results.1 = (bf16[4,4096]{1,0:T(4,128)(2,1)}, f32[16,512]{1,0:T(8,128)}, bf16[1024,256]{1,0:T(8,128)(2,1)}) custom-call(bf16[4,4096]{1,0:T(4,128)(2,1)} %get-tuple-element.9.refs_0_, f32[16,512]{1,0:T(8,128)} %get-tuple-element.10.refs_1_, bf16[1024,256]{1,0:T(8,128)(2,1)} %get-tuple-element.11.refs_2_), custom_call_target="tpu_custom_call" | custom-call | tf_op jit(solution)/shard_map/results/pallas_call | solution.py:848
